TPU v7x, 256 devices: a whole 4x4x8 slice. The times are simulated.
256 devices in a mesh: ctx: 32 (over y_lo, z, core), tp: 8 (over x, y_hi).
Axes of the slice: x: 4, y: 4 (y_hi: 2, y_lo: 2; y = y_hi * 2 + y_lo), z: 8, core: 2. Of those that a mesh axis runs over, the one named last changes fastest.
Arguments:
- queries: bfloat16 [4096, 8192], P('ctx', 'tp'), may hold values from -6 to 6
- keys_values: bfloat16 [4096, 1024], P('ctx', 'tp'), may hold values from -6 to 6
- forward_out: bfloat16 [4096, 8192], P('ctx', 'tp'), may hold values from -6 to 6
- out_grad: bfloat16 [4096, 8192], P('ctx', 'tp'), may hold values from -6 to 6
- kv_weight: bfloat16 [14848, 1024], P(None, 'tp'), may hold values from -3 to 3
- span_table: int32 [64], replicated, may hold values from 0 to 63, each once
Outputs:
- query_grad: bfloat16 [4096, 8192], P('ctx', 'tp')
- input_grad: bfloat16 [4096, 14848], P('ctx', 'tp')
Inputs may be any that keep to these rules, and one draw needn't show every extreme that they name: `span_table`: a permutation: every sequence block appears once.
All inputs are finite; a program needn't handle non-finite values.
Results may differ from a plain program's by a relative error of at most 0.0057.
Values may be sent and summed in bfloat16 or wider, within the bound.
No kernel may reach another device: no remote copies, remote signals or barrier semaphores. Data moves between devices by JAX's collectives and lax.ppermute only.
A program may use at most 64 MiB of HBM per device.

v0:
```python
import jax
import jax.numpy as jnp
from jax import lax
from jax.sharding import PartitionSpec as P

HEAD = 64


softmax_scale = 0.125
masked_score = -1e30


def passed_along(value, axis, steps):
    count = lax.axis_size(axis)
    pairs = [(source, (source + steps) % count) for source in range(count)]
    return lax.ppermute(value, axis, pairs)


def key_positions(first_row, row_count, span_table, span_rows):
    row_ids = first_row + jnp.arange(row_count, dtype=jnp.int32)
    blocks = row_ids // span_rows
    onehot = blocks[:, None] == jnp.arange(span_table.shape[0], dtype=jnp.int32)[None, :]
    starts = jnp.sum(jnp.where(onehot, span_table[None, :], 0), axis=1)
    return starts * span_rows + row_ids % span_rows


def block_scores(query_heads, key_rows, query_pos, key_pos):
    scores = (
        jnp.einsum("qhd,kd->hqk", query_heads, key_rows, preferred_element_type=jnp.float32)
        * softmax_scale
    )
    visible = (key_pos[None, :] <= query_pos[:, None])[None]
    return (jnp.where(visible, scores, masked_score), visible)


def on_device(queries, keys_values, forward_out, out_grad, kv_weight, span_table):
    tokens = queries.shape[0]
    span_rows = tokens // 2
    head_count = queries.shape[1] // HEAD
    cycle_index = lax.axis_index("ctx")
    cycle_size = lax.axis_size("ctx")
    query_pos = key_positions(cycle_index * tokens, tokens, span_table, span_rows)
    query_heads = queries.reshape(tokens, head_count, HEAD)
    grad_heads = out_grad.reshape(tokens, head_count, HEAD)
    forward_heads = forward_out.reshape(tokens, head_count, HEAD)
    grad_dot = jnp.sum(grad_heads.astype(jnp.float32) * forward_heads.astype(jnp.float32), axis=2).T
    gathered = lax.all_gather(keys_values, "ctx", axis=0, tiled=True)
    total_rows = gathered.shape[0]
    block_rows = min(512, total_rows)
    block_ids = jnp.arange(total_rows // block_rows, dtype=jnp.int32)

    def stats_step(running, block_index):
        row_top, row_total = running
        first_row = block_index * block_rows
        rows_block = lax.dynamic_slice_in_dim(gathered, first_row, block_rows, 0)
        key_pos = key_positions(first_row, block_rows, span_table, span_rows)
        scores, visible = block_scores(query_heads, rows_block[:, :HEAD], query_pos, key_pos)
        new_top = jnp.maximum(row_top, jnp.max(scores, axis=2))
        block_total = jnp.sum(
            jnp.where(visible, jnp.exp(scores - new_top[:, :, None]), 0.0), axis=2
        )
        row_total = row_total * jnp.exp(row_top - new_top) + block_total
        return ((new_top, row_total), None)

    start_top = jnp.full((head_count, tokens), masked_score, jnp.float32)
    start_total = jnp.zeros((head_count, tokens), jnp.float32)
    (row_top, row_total), _ = lax.scan(stats_step, (start_top, start_total), block_ids)
    log_total = row_top + jnp.log(row_total)

    def key_grads(first_row, row_count):
        rows_block = lax.dynamic_slice_in_dim(gathered, first_row, row_count, 0)
        key_rows = rows_block[:, :HEAD]
        value_rows = rows_block[:, HEAD:]
        key_pos = key_positions(first_row, row_count, span_table, span_rows)
        scores, visible = block_scores(query_heads, key_rows, query_pos, key_pos)
        probabilities = jnp.where(visible, jnp.exp(scores - log_total[:, :, None]), 0.0)
        weights = probabilities.astype(jnp.bfloat16)
        dprobs = jnp.einsum(
            "qhd,kd->hqk", grad_heads, value_rows, preferred_element_type=jnp.float32
        )
        dscores = (probabilities * (dprobs - grad_dot[:, :, None])).astype(jnp.bfloat16)
        query_add = jnp.einsum("hqk,kd->qhd", dscores, key_rows, preferred_element_type=jnp.float32)
        key_add = (
            jnp.einsum("hqk,qhd->kd", dscores, query_heads, preferred_element_type=jnp.float32)
            * softmax_scale
        )
        value_add = jnp.einsum(
            "hqk,qhd->kd", weights, grad_heads, preferred_element_type=jnp.float32
        )
        return (query_add, jnp.concatenate([key_add, value_add], axis=1))

    query_start = jnp.zeros((tokens, head_count, HEAD), jnp.float32)

    def travel_step(turn_index, running):
        query_sum, carried = running
        owner_block = (cycle_index - turn_index) % cycle_size
        query_add, own_add = key_grads(owner_block * tokens, tokens)
        carried = passed_along(carried + own_add, "ctx", 1)
        return (query_sum + query_add, carried)

    carried_start = jnp.zeros((tokens, 2 * HEAD), jnp.float32)
    query_sum, kv_sum = lax.fori_loop(0, cycle_size, travel_step, (query_start, carried_start))
    query_grad = (query_sum * softmax_scale).astype(jnp.bfloat16).reshape(tokens, head_count * HEAD)
    kv_grad = kv_sum.astype(jnp.bfloat16)
    partial_terms = lax.dot_general(
        kv_grad, kv_weight, (((1,), (1,)), ((), ())), preferred_element_type=jnp.float32
    )
    input_grad = lax.psum_scatter(partial_terms, "tp", scatter_dimension=1, tiled=True)
    return (query_grad, input_grad.astype(jnp.bfloat16))


def solution(mesh):
    placed = (P("ctx", "tp"), P("ctx", "tp"), P("ctx", "tp"), P("ctx", "tp"), P(None, "tp"), P())
    return jax.shard_map(
        on_device,
        mesh=mesh,
        in_specs=placed,
        out_specs=(P("ctx", "tp"), P("ctx", "tp")),
        check_vma=False,
    )
```

profile of v0, /device:TPU:32, one launch (start us, length us, event | category | flops | bytes accessed | tf_op | source)
XLA Modules:
  0.0 546.5 jit_solution(8518143127407360794)
XLA Ops:
  13.0 62.2 %all-gather.2.cloned.1.call-done = bf16[4096,128]{0,1:T(8,128)(2,1)} async-done(((bf16[128,128]{0,1:T(8,128)(2,1)}), bf16[4096,128]{0,1:T(8,128)(2,1)}) %all-gather.2.cloned.1.call-update) | async-done | bytes 1048592 | tf_op jit(solution)/shard_map/all_gather | solution.py:47
  75.2 38.5 %while.34 = (s32[]{:T(128)}, f32[16,128]{1,0:T(8,128)S(1)}, f32[16,128]{1,0:T(8,128)S(1)}, s32[8]{0:T(128)S(1)}, s32[64]{0:T(128)}, /*index=5*/s32[128]{0:T(128)...) while((s32[]{:T(128)}, f32[16,128]{1,0:T(8,128)S(1)}, ...), condition=%wide.region_5.6_spmd.clone, body=%wide.region_1.5_spmd.clone.sunk | while | flops 142795264 | bytes 9032654 | solution.py:67
  113.7 298.0 %while.35 = (s32[]{:T(128)}, f32[128,16,64]{0,2,1:T(8,128)S(1)}, f32[128,128]{0,1:T(8,128)S(1)}, s32[]{:T(128)}, bf16[4096,128]{0,1:T(8,128)(2,1)}, /*index=5*/s...) while((s32[]{:T(128)}, f32[128,16,64]{0,2,1:T(8,128)S(1)}, ...), condition=%wide.region_9.10_spmd.clone, body=%wide.region_7.9_spmd.clone.sunk | while | flops 170217104 | bytes 7442594 | solution.py:102
  148.6 4.8 collective-permute-done
  158.2 4.8 collective-permute-done
  167.8 4.8 collective-permute-done
  177.3 4.8 collective-permute-done
  186.9 4.9 collective-permute-done
  206.1 4.8 collective-permute-done
  215.6 4.8 collective-permute-done
  244.3 4.8 collective-permute-done
  253.9 4.8 collective-permute-done
  263.5 4.8 collective-permute-done
  273.0 4.8 collective-permute-done
  282.6 4.8 collective-permute-done
  292.2 4.8 collective-permute-done
  301.7 4.8 collective-permute-done
  311.3 4.8 collective-permute-done
  320.9 4.8 collective-permute-done
  330.4 4.8 collective-permute-done
  368.7 4.8 collective-permute-done
  378.3 4.8 collective-permute-done
  411.7 6.2 %fusion.22 = f32[128,14848]{0,1:T(8,128)} fusion(bf16[14848,128]{1,0:T(8,128)(2,1)} %param.14, f32[128,128]{0,1:T(8,128)S(1)} %get-tuple-element.415), kind=kOutput, calls=%fused_computation.56 | convolution fusion | flops 486555648 | bytes 11468800 | tf_op jit(solution)/shard_map/dot_general | solution.py:105
  418.9 118.7 %reduce-scatter.2.cloned.1.call-done = f32[128,1856]{0,1:T(8,128)} async-done(((f32[128,14848]{0,1:T(8,128)}), f32[128,1856]{0,1:T(8,128)}) %reduce-scatter.2.cloned.1.call-update) | async-done | bytes 950288 | tf_op jit(solution)/shard_map/reduce_scatter | solution.py:108
  (466 shorter events, 246.3 us)
Async XLA Ops:
  7.2 68.1 %all-gather.2.cloned.1.call-start = ((), (), s32[]{:S(2)}) async-start(), calls=%async_computation.1 | async-start | bytes 1081344 | tf_op jit(solution)/shard_map/all_gather | solution.py:47
  8.7 528.9 %reduce-scatter.2.cloned.1.call-start = ((), (), s32[]{:S(2)}) async-start(), calls=%async_computation.2 | async-start | bytes 8552448 | tf_op jit(solution)/shard_map/reduce_scatter | solution.py:108
  147.5 5.9 %collective-permute-start = (f32[128,128]{0,1:T(8,128)S(1)}, f32[128,128]{0,1:T(8,128)S(1)}, u32[]{:S(2)}, u32[]{:S(2)}) collective-permute-start(f32[128,128]{0,1:T(8,128)S(1)} %maximum_add_fusion.2), channel_id=1, source_target_pairs={{0,8},{8,16},{16,24},{24,32},{32,40},{40,48},{48,56},{56,64},{64,7... | collective-permute-start | bytes 196616 | tf_op jit(solution)/shard_map/while/body/eval_jaxpr/ppermute | solution.py:16
  157.1 5.9 %collective-permute-start = (f32[128,128]{0,1:T(8,128)S(1)}, f32[128,128]{0,1:T(8,128)S(1)}, u32[]{:S(2)}, u32[]{:S(2)}) collective-permute-start(f32[128,128]{0,1:T(8,128)S(1)} %maximum_add_fusion.2), channel_id=1, source_target_pairs={{0,8},{8,16},{16,24},{24,32},{32,40},{40,48},{48,56},{56,64},{64,7... | collective-permute-start | bytes 196616 | tf_op jit(solution)/shard_map/while/body/eval_jaxpr/ppermute | solution.py:16
  166.7 5.9 %collective-permute-start = (f32[128,128]{0,1:T(8,128)S(1)}, f32[128,128]{0,1:T(8,128)S(1)}, u32[]{:S(2)}, u32[]{:S(2)}) collective-permute-start(f32[128,128]{0,1:T(8,128)S(1)} %maximum_add_fusion.2), channel_id=1, source_target_pairs={{0,8},{8,16},{16,24},{24,32},{32,40},{40,48},{48,56},{56,64},{64,7... | collective-permute-start | bytes 196616 | tf_op jit(solution)/shard_map/while/body/eval_jaxpr/ppermute | solution.py:16
  176.2 5.9 %collective-permute-start = (f32[128,128]{0,1:T(8,128)S(1)}, f32[128,128]{0,1:T(8,128)S(1)}, u32[]{:S(2)}, u32[]{:S(2)}) collective-permute-start(f32[128,128]{0,1:T(8,128)S(1)} %maximum_add_fusion.2), channel_id=1, source_target_pairs={{0,8},{8,16},{16,24},{24,32},{32,40},{40,48},{48,56},{56,64},{64,7... | collective-permute-start | bytes 196616 | tf_op jit(solution)/shard_map/while/body/eval_jaxpr/ppermute | solution.py:16
  185.8 6.0 %collective-permute-start = (f32[128,128]{0,1:T(8,128)S(1)}, f32[128,128]{0,1:T(8,128)S(1)}, u32[]{:S(2)}, u32[]{:S(2)}) collective-permute-start(f32[128,128]{0,1:T(8,128)S(1)} %maximum_add_fusion.2), channel_id=1, source_target_pairs={{0,8},{8,16},{16,24},{24,32},{32,40},{40,48},{48,56},{56,64},{64,7... | collective-permute-start | bytes 196616 | tf_op jit(solution)/shard_map/while/body/eval_jaxpr/ppermute | solution.py:16
  205.0 5.9 %collective-permute-start = (f32[128,128]{0,1:T(8,128)S(1)}, f32[128,128]{0,1:T(8,128)S(1)}, u32[]{:S(2)}, u32[]{:S(2)}) collective-permute-start(f32[128,128]{0,1:T(8,128)S(1)} %maximum_add_fusion.2), channel_id=1, source_target_pairs={{0,8},{8,16},{16,24},{24,32},{32,40},{40,48},{48,56},{56,64},{64,7... | collective-permute-start | bytes 196616 | tf_op jit(solution)/shard_map/while/body/eval_jaxpr/ppermute | solution.py:16
  214.5 5.9 %collective-permute-start = (f32[128,128]{0,1:T(8,128)S(1)}, f32[128,128]{0,1:T(8,128)S(1)}, u32[]{:S(2)}, u32[]{:S(2)}) collective-permute-start(f32[128,128]{0,1:T(8,128)S(1)} %maximum_add_fusion.2), channel_id=1, source_target_pairs={{0,8},{8,16},{16,24},{24,32},{32,40},{40,48},{48,56},{56,64},{64,7... | collective-permute-start | bytes 196616 | tf_op jit(solution)/shard_map/while/body/eval_jaxpr/ppermute | solution.py:16
  243.2 5.9 %collective-permute-start = (f32[128,128]{0,1:T(8,128)S(1)}, f32[128,128]{0,1:T(8,128)S(1)}, u32[]{:S(2)}, u32[]{:S(2)}) collective-permute-start(f32[128,128]{0,1:T(8,128)S(1)} %maximum_add_fusion.2), channel_id=1, source_target_pairs={{0,8},{8,16},{16,24},{24,32},{32,40},{40,48},{48,56},{56,64},{64,7... | collective-permute-start | bytes 196616 | tf_op jit(solution)/shard_map/while/body/eval_jaxpr/ppermute | solution.py:16
  252.8 5.9 %collective-permute-start = (f32[128,128]{0,1:T(8,128)S(1)}, f32[128,128]{0,1:T(8,128)S(1)}, u32[]{:S(2)}, u32[]{:S(2)}) collective-permute-start(f32[128,128]{0,1:T(8,128)S(1)} %maximum_add_fusion.2), channel_id=1, source_target_pairs={{0,8},{8,16},{16,24},{24,32},{32,40},{40,48},{48,56},{56,64},{64,7... | collective-permute-start | bytes 196616 | tf_op jit(solution)/shard_map/while/body/eval_jaxpr/ppermute | solution.py:16
  262.4 5.9 %collective-permute-start = (f32[128,128]{0,1:T(8,128)S(1)}, f32[128,128]{0,1:T(8,128)S(1)}, u32[]{:S(2)}, u32[]{:S(2)}) collective-permute-start(f32[128,128]{0,1:T(8,128)S(1)} %maximum_add_fusion.2), channel_id=1, source_target_pairs={{0,8},{8,16},{16,24},{24,32},{32,40},{40,48},{48,56},{56,64},{64,7... | collective-permute-start | bytes 196616 | tf_op jit(solution)/shard_map/while/body/eval_jaxpr/ppermute | solution.py:16
  271.9 5.9 %collective-permute-start = (f32[128,128]{0,1:T(8,128)S(1)}, f32[128,128]{0,1:T(8,128)S(1)}, u32[]{:S(2)}, u32[]{:S(2)}) collective-permute-start(f32[128,128]{0,1:T(8,128)S(1)} %maximum_add_fusion.2), channel_id=1, source_target_pairs={{0,8},{8,16},{16,24},{24,32},{32,40},{40,48},{48,56},{56,64},{64,7... | collective-permute-start | bytes 196616 | tf_op jit(solution)/shard_map/while/body/eval_jaxpr/ppermute | solution.py:16
  281.5 5.9 %collective-permute-start = (f32[128,128]{0,1:T(8,128)S(1)}, f32[128,128]{0,1:T(8,128)S(1)}, u32[]{:S(2)}, u32[]{:S(2)}) collective-permute-start(f32[128,128]{0,1:T(8,128)S(1)} %maximum_add_fusion.2), channel_id=1, source_target_pairs={{0,8},{8,16},{16,24},{24,32},{32,40},{40,48},{48,56},{56,64},{64,7... | collective-permute-start | bytes 196616 | tf_op jit(solution)/shard_map/while/body/eval_jaxpr/ppermute | solution.py:16
  291.1 5.9 %collective-permute-start = (f32[128,128]{0,1:T(8,128)S(1)}, f32[128,128]{0,1:T(8,128)S(1)}, u32[]{:S(2)}, u32[]{:S(2)}) collective-permute-start(f32[128,128]{0,1:T(8,128)S(1)} %maximum_add_fusion.2), channel_id=1, source_target_pairs={{0,8},{8,16},{16,24},{24,32},{32,40},{40,48},{48,56},{56,64},{64,7... | collective-permute-start | bytes 196616 | tf_op jit(solution)/shard_map/while/body/eval_jaxpr/ppermute | solution.py:16
  300.6 5.9 %collective-permute-start = (f32[128,128]{0,1:T(8,128)S(1)}, f32[128,128]{0,1:T(8,128)S(1)}, u32[]{:S(2)}, u32[]{:S(2)}) collective-permute-start(f32[128,128]{0,1:T(8,128)S(1)} %maximum_add_fusion.2), channel_id=1, source_target_pairs={{0,8},{8,16},{16,24},{24,32},{32,40},{40,48},{48,56},{56,64},{64,7... | collective-permute-start | bytes 196616 | tf_op jit(solution)/shard_map/while/body/eval_jaxpr/ppermute | solution.py:16
  310.2 5.9 %collective-permute-start = (f32[128,128]{0,1:T(8,128)S(1)}, f32[128,128]{0,1:T(8,128)S(1)}, u32[]{:S(2)}, u32[]{:S(2)}) collective-permute-start(f32[128,128]{0,1:T(8,128)S(1)} %maximum_add_fusion.2), channel_id=1, source_target_pairs={{0,8},{8,16},{16,24},{24,32},{32,40},{40,48},{48,56},{56,64},{64,7... | collective-permute-start | bytes 196616 | tf_op jit(solution)/shard_map/while/body/eval_jaxpr/ppermute | solution.py:16
  319.8 5.9 %collective-permute-start = (f32[128,128]{0,1:T(8,128)S(1)}, f32[128,128]{0,1:T(8,128)S(1)}, u32[]{:S(2)}, u32[]{:S(2)}) collective-permute-start(f32[128,128]{0,1:T(8,128)S(1)} %maximum_add_fusion.2), channel_id=1, source_target_pairs={{0,8},{8,16},{16,24},{24,32},{32,40},{40,48},{48,56},{56,64},{64,7... | collective-permute-start | bytes 196616 | tf_op jit(solution)/shard_map/while/body/eval_jaxpr/ppermute | solution.py:16
  329.3 5.9 %collective-permute-start = (f32[128,128]{0,1:T(8,128)S(1)}, f32[128,128]{0,1:T(8,128)S(1)}, u32[]{:S(2)}, u32[]{:S(2)}) collective-permute-start(f32[128,128]{0,1:T(8,128)S(1)} %maximum_add_fusion.2), channel_id=1, source_target_pairs={{0,8},{8,16},{16,24},{24,32},{32,40},{40,48},{48,56},{56,64},{64,7... | collective-permute-start | bytes 196616 | tf_op jit(solution)/shard_map/while/body/eval_jaxpr/ppermute | solution.py:16
  338.9 5.9 %collective-permute-start = (f32[128,128]{0,1:T(8,128)S(1)}, f32[128,128]{0,1:T(8,128)S(1)}, u32[]{:S(2)}, u32[]{:S(2)}) collective-permute-start(f32[128,128]{0,1:T(8,128)S(1)} %maximum_add_fusion.2), channel_id=1, source_target_pairs={{0,8},{8,16},{16,24},{24,32},{32,40},{40,48},{48,56},{56,64},{64,7... | collective-permute-start | bytes 196616 | tf_op jit(solution)/shard_map/while/body/eval_jaxpr/ppermute | solution.py:16
  358.0 5.9 %collective-permute-start = (f32[128,128]{0,1:T(8,128)S(1)}, f32[128,128]{0,1:T(8,128)S(1)}, u32[]{:S(2)}, u32[]{:S(2)}) collective-permute-start(f32[128,128]{0,1:T(8,128)S(1)} %maximum_add_fusion.2), channel_id=1, source_target_pairs={{0,8},{8,16},{16,24},{24,32},{32,40},{40,48},{48,56},{56,64},{64,7... | collective-permute-start | bytes 196616 | tf_op jit(solution)/shard_map/while/body/eval_jaxpr/ppermute | solution.py:16
  367.6 5.9 %collective-permute-start = (f32[128,128]{0,1:T(8,128)S(1)}, f32[128,128]{0,1:T(8,128)S(1)}, u32[]{:S(2)}, u32[]{:S(2)}) collective-permute-start(f32[128,128]{0,1:T(8,128)S(1)} %maximum_add_fusion.2), channel_id=1, source_target_pairs={{0,8},{8,16},{16,24},{24,32},{32,40},{40,48},{48,56},{56,64},{64,7... | collective-permute-start | bytes 196616 | tf_op jit(solution)/shard_map/while/body/eval_jaxpr/ppermute | solution.py:16
  377.2 5.9 %collective-permute-start = (f32[128,128]{0,1:T(8,128)S(1)}, f32[128,128]{0,1:T(8,128)S(1)}, u32[]{:S(2)}, u32[]{:S(2)}) collective-permute-start(f32[128,128]{0,1:T(8,128)S(1)} %maximum_add_fusion.2), channel_id=1, source_target_pairs={{0,8},{8,16},{16,24},{24,32},{32,40},{40,48},{48,56},{56,64},{64,7... | collective-permute-start | bytes 196616 | tf_op jit(solution)/shard_map/while/body/eval_jaxpr/ppermute | solution.py:16
  405.9 5.9 %collective-permute-start = (f32[128,128]{0,1:T(8,128)S(1)}, f32[128,128]{0,1:T(8,128)S(1)}, u32[]{:S(2)}, u32[]{:S(2)}) collective-permute-start(f32[128,128]{0,1:T(8,128)S(1)} %maximum_add_fusion.2), channel_id=1, source_target_pairs={{0,8},{8,16},{16,24},{24,32},{32,40},{40,48},{48,56},{56,64},{64,7... | collective-permute-start | bytes 196616 | tf_op jit(solution)/shard_map/while/body/eval_jaxpr/ppermute | solution.py:16
  (10 other events, 50.5 us)
Sparse Core Ops, SparseCore 0:
  10.3 64.8 all-gather.1
  418.1 119.4 reduce-scatter.1
where the time goes:
time: 553 us; the launch traced here: 546 us
  waiting for transfers between devices  325 us (59%)
  matrix products  140 us (25%)
  other arithmetic  46.1 us (8%)
  between operations  14.1 us (3%)
  local copies, waits for them, and re-layouts  10.4 us (2%)
  loops' own time  8.02 us (1%)
    ppermute x32, waiting for transfers between devices, passed_along(): return lax.ppermute(value, axis, pairs)  144 us
    reduce_scatter x1, waiting for transfers between devices, on_device(): lax.psum_scatter(partial_terms, 'tp', scatter_dimension=1, tiled=True)  119 us
    all_gather x1, waiting for transfers between devices, on_device(): gathered = lax.all_gather(keys_values, 'ctx', axis=0, tiled=True)  62.2 us
    dot_general x40, matrix products, block_scores(): jnp.einsum('qhd,kd->hqk', query_heads, key_rows, preferred_element_type=j...  48.8 us
    dot_general x32, matrix products, key_grads(): jnp.einsum('qhd,kd->hqk', grad_heads, value_rows, preferred_element_type=...  33.4 us
    dot_general x32, matrix products, key_grads(): jnp.einsum('hqk,kd->qhd', dscores, key_rows, preferred_element_type=jnp.f...  32.1 us
    reduce_sum x41, other arithmetic, key_positions(): starts = jnp.sum(jnp.where(onehot, span_table[None, :], 0), axis=1)  30.7 us
  transfers between devices with their start and end apart: 34, of which 34 were waited for; matrix products, arithmetic and copies ran while one was open for 7% of the time, Pallas kernels for 0%

commit v1 on v0

v1 whole, which is shorter than its diff:
```python
import functools

import jax
import jax.numpy as jnp
from jax import lax
from jax.experimental import pallas as pl
from jax.experimental.pallas import tpu as pltpu
from jax.sharding import PartitionSpec as P

HEAD = 64
SPAN = 64
BLOCK = 256
PAIR = 2 * HEAD
SCALE = 0.125
LOG2E = 1.4426950408889634
MASKED = -1e30

f32 = jnp.float32
bf16 = jnp.bfloat16


def dot_t(a, b):
    return lax.dot_general(a, b, (((1,), (1,)), ((), ())), preferred_element_type=f32)


def dot(a, b):
    return lax.dot_general(a, b, (((1,), (0,)), ((), ())), preferred_element_type=f32)


def swap_halves(x):
    return pltpu.roll(x.astype(f32), HEAD, 1)


def attention_kernel(
    slot_pos,
    my_pos,
    kv_a,
    kv_b,
    rows_a,
    rows_b,
    dq_a,
    dq_b,
    dkv_a,
    dkv_b,
    kv_sorted,
    kk,
    va,
    av,
    kt,
    scores,
    acc1,
    acc2,
    dqt,
):
    half_slots = kv_a.shape[0]
    blocks = kk.shape[0]
    per_block = BLOCK // SPAN
    width = dq_a.shape[1]
    pairs = width // PAIR
    qcount = pairs * SPAN

    def place(slot, _):
        for which, src in enumerate((kv_a, kv_b)):
            p = slot_pos[which * half_slots + slot]
            row = pl.multiple_of((p % per_block) * SPAN, SPAN)
            kv_sorted[p // per_block, pl.ds(row, SPAN), :] = src[slot]
        return 0

    lax.fori_loop(0, half_slots, place, 0)

    lane_k = lax.broadcasted_iota(jnp.int32, (BLOCK, PAIR), 1)
    low_k = lane_k < HEAD

    def prepare(b, _):
        kv = kv_sorted[b].astype(f32)
        vk = pltpu.roll(kv, HEAD, 1)
        kk[b] = jnp.where(low_k, kv, vk).astype(bf16)
        ones_hi = ((lane_k >= HEAD) & (lane_k < HEAD + 3)).astype(f32)
        ones_lo = (lane_k < 3).astype(f32)
        va[b] = jnp.where(low_k, vk, ones_hi).astype(bf16)
        av[b] = jnp.where(low_k, ones_lo, kv).astype(bf16)
        kt[b] = jnp.transpose(kv)[:HEAD].astype(bf16)
        acc1[b] = jnp.zeros((BLOCK, PAIR), f32)
        acc2[b] = jnp.zeros((BLOCK, PAIR), f32)
        return 0

    lax.fori_loop(0, blocks, prepare, 0)

    lane_q = lax.broadcasted_iota(jnp.int32, (qcount, PAIR), 1)
    low_q = lane_q < HEAD
    key_row = lax.broadcasted_iota(jnp.int32, (BLOCK, qcount), 0)
    query_row = lax.broadcasted_iota(jnp.int32, (BLOCK, qcount), 1) % SPAN

    def one_span(pos, rows, row, dq_out):
        def stacked(part):
            return jnp.concatenate(
                [
                    rows[pl.ds(row, SPAN), part * width + p * PAIR : part * width + (p + 1) * PAIR]
                    for p in range(pairs)
                ],
                axis=0,
            )

        q = stacked(0)
        do = stacked(1)
        fo = stacked(2)
        qf = q.astype(f32)
        dof = do.astype(f32)
        q2 = qf * (SCALE * LOG2E)
        hi = q2.astype(bf16).astype(f32)
        lo_rolled = pltpu.roll(q2 - hi, HEAD, 1)
        q_e = jnp.where(low_q, hi, lo_rolled).astype(bf16)
        q_o = jnp.where(low_q, lo_rolled, hi).astype(bf16)
        prod = dof * fo.astype(f32)

        def parts(d):
            d = -d
            a = d.astype(bf16).astype(f32)
            b = (d - a).astype(bf16).astype(f32)
            return a, b, d - a - b

        def with_parts(d, base, keep):
            a, b, c = parts(d)
            at = 0 if keep else HEAD
            aux = jnp.where(lane_q == at, a, jnp.where(lane_q == at + 1, b, jnp.where(lane_q == at + 2, c, 0.0)))
            return jnp.where(low_q != keep, base, aux).astype(bf16)

        d_e = jnp.sum(jnp.where(low_q, prod, 0.0), axis=1, keepdims=True)
        d_o = jnp.sum(jnp.where(low_q, 0.0, prod), axis=1, keepdims=True)
        do_e = with_parts(d_e, dof, False)
        do_o = with_parts(d_o, dof, True)
        zero = jnp.zeros_like(qf)
        qe0 = jnp.where(low_q, qf, zero).astype(bf16)
        q0o = jnp.where(low_q, zero, qf).astype(bf16)
        doe0 = jnp.where(low_q, dof, zero).astype(bf16)
        do0o = jnp.where(low_q, zero, dof).astype(bf16)

        last = pos // per_block

        def stats(b, running, masked):
            new = []
            for e, qq in enumerate((q_e, q_o)):
                m, l = running[e]
                s = dot_t(kk[b], qq)
                if masked:
                    s = jnp.where(key_row <= (pos % per_block) * SPAN + query_row, s, MASKED)
                scores[b, :, e * qcount : (e + 1) * qcount] = s
                top = jnp.maximum(m, jnp.max(s, axis=0, keepdims=True))
                l = l * jnp.exp2(m - top) + jnp.sum(jnp.exp2(s - top), axis=0, keepdims=True)
                new.append((top, l))
            return tuple(new)

        init = (jnp.full((1, qcount), MASKED, f32), jnp.zeros((1, qcount), f32))
        running = lax.fori_loop(0, last, functools.partial(stats, masked=False), (init, init))
        running = stats(last, running, True)
        lse = [m + jnp.log2(l) for m, l in running]

        dqt[...] = jnp.zeros_like(dqt)

        def grads(b, _):
            ps, dss = [], []
            for e, (v, dd) in enumerate(((va, do_e), (av, do_o))):
                p = jnp.exp2(scores[b, :, e * qcount : (e + 1) * qcount] - lse[e])
                dp = dot_t(v[b], dd)
                ps.append(p.astype(bf16))
                dss.append((p * dp).astype(bf16))
            acc1[b] += dot(dss[0], qe0) + dot(ps[1], do0o)
            acc2[b] += dot(dss[1], q0o) + dot(ps[0], doe0)
            dqt[0:HEAD] += dot(kt[b], dss[0])
            dqt[HEAD:PAIR] += dot(kt[b], dss[1])
            return 0

        lax.fori_loop(0, last + 1, grads, 0)
        dq = (jnp.transpose(dqt[...]) * SCALE).astype(bf16)
        for p in range(pairs):
            dq_out[pl.ds(row, SPAN), p * PAIR : (p + 1) * PAIR] = dq[p * SPAN : (p + 1) * SPAN]

    for which, (rows, dq_out) in enumerate(((rows_a, dq_a), (rows_b, dq_b))):
        spans = rows.shape[0] // SPAN

        def step(i, _):
            one_span(my_pos[which * spans + i], rows, pl.multiple_of(i * SPAN, SPAN), dq_out)
            return 0

        lax.fori_loop(0, spans, step, 0)

    lane_s = lax.broadcasted_iota(jnp.int32, (SPAN, PAIR), 1)
    factor = jnp.where(lane_s < HEAD, SCALE, 1.0)

    def collect(slot, _):
        for which, dst in enumerate((dkv_a, dkv_b)):
            p = slot_pos[which * half_slots + slot]
            row = pl.multiple_of((p % per_block) * SPAN, SPAN)
            a1 = acc1[p // per_block, pl.ds(row, SPAN), :]
            a2 = acc2[p // per_block, pl.ds(row, SPAN), :]
            dst[slot] = ((a1 + pltpu.roll(a2, HEAD, 1)) * factor).astype(bf16)
        return 0

    lax.fori_loop(0, half_slots, collect, 0)


def attention_grads(slot_pos, my_pos, kv_a, kv_b, rows_a, rows_b):
    slots = 2 * kv_a.shape[0]
    blocks = slots * SPAN // BLOCK
    width = rows_a.shape[1] // 3
    qcount = width // PAIR * SPAN
    smem = pl.BlockSpec(memory_space=pltpu.SMEM)
    vmem = pl.BlockSpec(memory_space=pltpu.VMEM)
    tokens = rows_a.shape[0]
    pairs_of = slots * SPAN * tokens * 2 * width // HEAD
    return pl.pallas_call(
        attention_kernel,
        out_shape=(
            jax.ShapeDtypeStruct((tokens, width), bf16),
            jax.ShapeDtypeStruct((tokens, width), bf16),
            jax.ShapeDtypeStruct(kv_a.shape, bf16),
            jax.ShapeDtypeStruct(kv_b.shape, bf16),
        ),
        in_specs=[smem, smem, vmem, vmem, vmem, vmem],
        out_specs=(vmem, vmem, vmem, vmem),
        scratch_shapes=[
            pltpu.VMEM((blocks, BLOCK, PAIR), bf16),
            pltpu.VMEM((blocks, BLOCK, PAIR), bf16),
            pltpu.VMEM((blocks, BLOCK, PAIR), bf16),
            pltpu.VMEM((blocks, BLOCK, PAIR), bf16),
            pltpu.VMEM((blocks, HEAD, BLOCK), bf16),
            pltpu.VMEM((blocks, BLOCK, 2 * qcount), f32),
            pltpu.VMEM((blocks, BLOCK, PAIR), f32),
            pltpu.VMEM((blocks, BLOCK, PAIR), f32),
            pltpu.VMEM((PAIR, qcount), f32),
        ],
        compiler_params=pltpu.CompilerParams(vmem_limit_bytes=48 * 1024 * 1024),
        cost_estimate=pl.CostEstimate(
            flops=pairs_of * HEAD * 2 * 5 * 4, bytes_accessed=6 << 20, transcendentals=pairs_of
        ),
    )(slot_pos, my_pos, kv_a, kv_b, rows_a, rows_b)


def project_kernel(kv_ref, w_ref, out_ref):
    total = dot_t(kv_ref[0], w_ref[0])
    for g in range(1, kv_ref.shape[0]):
        total = total + dot_t(kv_ref[g], w_ref[g])
    out_ref[...] = total.astype(bf16)


def project(kv, w):
    vmem = pl.BlockSpec(memory_space=pltpu.VMEM)
    return pl.pallas_call(
        project_kernel,
        out_shape=jax.ShapeDtypeStruct((kv.shape[1], w.shape[1]), bf16),
        in_specs=[vmem, vmem],
        out_specs=vmem,
        compiler_params=pltpu.CompilerParams(vmem_limit_bytes=32 * 1024 * 1024),
        cost_estimate=pl.CostEstimate(
            flops=2 * kv.size * w.shape[1], bytes_accessed=2 * w.size, transcendentals=0
        ),
    )(kv, w)


def on_device(queries, keys_values, forward_out, out_grad, kv_weight, span_table):
    tokens = queries.shape[0]
    half = queries.shape[1] // 2
    me = lax.axis_index("ctx")
    core = me % 2
    count = lax.axis_size("ctx")
    groups = lax.axis_size("tp")
    chips = count // 2
    same_core = [[2 * chip + k for chip in range(chips)] for k in range(2)]
    other_core = [(i, i ^ 1) for i in range(count)]

    def to_all(x, n):
        return jnp.broadcast_to(x[None], (n,) + x.shape)

    def exchanged(x):
        return lax.ppermute(x, "ctx", other_core)

    features = kv_weight.shape[0] // groups
    weight = lax.all_to_all(kv_weight.reshape(groups, features, kv_weight.shape[1]), "tp", 0, 0)

    kv_a = lax.all_to_all(to_all(keys_values, chips), "ctx", 0, 0, axis_index_groups=same_core)
    kv_b = exchanged(kv_a)

    def my_heads(k):
        return [lax.dynamic_slice_in_dim(x, k * half, half, 1) for x in (queries, out_grad, forward_out)]

    rows_a = jnp.concatenate(my_heads(core), axis=1)
    rows_b = exchanged(jnp.concatenate(my_heads(1 - core), axis=1))

    spans = tokens // SPAN
    by_device = span_table.reshape(chips, 2, spans)
    mine = lax.dynamic_index_in_dim(by_device, core, 1, False)
    theirs = lax.dynamic_index_in_dim(by_device, 1 - core, 1, False)
    slot_pos = jnp.concatenate([mine.reshape(-1), theirs.reshape(-1)])
    chip = me // 2
    my_pos = jnp.concatenate(
        [
            lax.dynamic_index_in_dim(mine, chip, 0, False),
            lax.dynamic_index_in_dim(theirs, chip, 0, False),
        ]
    )

    by_span = (chips * spans, SPAN, keys_values.shape[1])
    dq_a, dq_b, dkv_a, dkv_b = attention_grads(
        slot_pos, my_pos, kv_a.reshape(by_span), kv_b.reshape(by_span), rows_a, rows_b
    )
    dkv = (dkv_a.astype(f32) + exchanged(dkv_b).astype(f32)).astype(bf16)
    terms = lax.all_to_all(
        dkv.reshape(chips, tokens, -1), "ctx", 0, 0, axis_index_groups=same_core
    )
    kv_grad = jnp.sum(terms.astype(f32), axis=0).astype(bf16)
    all_groups = lax.all_to_all(to_all(kv_grad, groups), "tp", 0, 0)
    input_grad = project(all_groups, weight)
    dq_other = exchanged(dq_b)
    query_grad = jnp.where(
        core == 0,
        jnp.concatenate([dq_a, dq_other], axis=1),
        jnp.concatenate([dq_other, dq_a], axis=1),
    )
    return query_grad, input_grad


def solution(mesh):
    placed = (P("ctx", "tp"), P("ctx", "tp"), P("ctx", "tp"), P("ctx", "tp"), P(None, "tp"), P())
    return jax.shard_map(
        on_device,
        mesh=mesh,
        in_specs=placed,
        out_specs=(P("ctx", "tp"), P("ctx", "tp")),
        check_vma=False,
    )
```

time: 553 us -> 169 us (0.31); the launches traced: 546 us -> 169 us
  waiting for transfers between devices: 325 us -> 66.4 us
  matrix products: 140 us -> 0 us
  other arithmetic: 46.1 us -> 1.25 us
  blocking collectives: 0 us -> 41.8 us
  Pallas kernels: 0 us -> 39.5 us
  between operations: 14.1 us -> 0.82 us
  starting transfers between devices: 2.95 us -> 14.5 us
  loops' own time: 8.02 us -> 0 us
    dot_general x169 -> x0, matrix products: 140 us -> none  [the longest x40 48.8 us: block_scores(): jnp.einsum('qhd,kd->hqk', query_heads, key_rows, preferred_element_type=j...]
    ppermute x32 -> x4, waiting for transfers between devices: 144 us -> 4.82 us  [exchanged(): return lax.ppermute(x, 'ctx', other_core)]
    reduce_scatter x1 -> x0, waiting for transfers between devices: 119 us -> none  [on_device(): lax.psum_scatter(partial_terms, 'tp', scatter_dimension=1, tiled=True)]
    all_gather x1 -> x0, waiting for transfers between devices: 62.2 us -> none  [on_device(): gathered = lax.all_gather(keys_values, 'ctx', axis=0, tiled=True)]
    all_to_all x0 -> x2, waiting for transfers between devices: none -> 61.6 us  [the longest x1 49.3 us: on_device(): lax.all_to_all(kv_weight.reshape(groups, features, kv_weight.shape[1]), '...]
    all_to_all x0 -> x2, blocking collectives: none -> 41.8 us  [the longest x1 26.9 us: on_device(): lax.all_to_all(dkv.reshape(chips, tokens, -1), 'ctx', 0, 0, axis_index_gr...]
    pallas_call x0 -> x2, Pallas kernels: none -> 39.5 us  [the longest x1 36.2 us: attention_grads(): pl.pallas_call(attention_kernel, out_shape=(jax.ShapeDtypeStruct((tokens,...]
    reduce_sum x50 -> x1, other arithmetic: 38.6 us -> 0.08 us  [on_device(): kv_grad = jnp.sum(terms.astype(f32), axis=0).astype(bf16)]
  transfers between devices with their start and end apart: 34 -> 6, of which waited for: 34 -> 5; matrix products, arithmetic and copies ran while one was open for 7% -> 2% of each run, Pallas kernels for 0% -> 0%
where the time goes in v1:
time: 169 us
  waiting for transfers between devices  66.4 us (39%)
  blocking collectives  41.8 us (25%)
  Pallas kernels  39.5 us (23%)
  starting transfers between devices  14.5 us (9%)
  local copies, waits for them, and re-layouts  5.15 us (3%)
    all_to_all x1, waiting for transfers between devices, on_device(): lax.all_to_all(kv_weight.reshape(groups, features, kv_weight.shape[1]), '...  49.3 us
    pallas_call x1, Pallas kernels, attention_grads(): pl.pallas_call(attention_kernel, out_shape=(jax.ShapeDtypeStruct((tokens,...  36.2 us
    all_to_all x1, blocking collectives, on_device(): lax.all_to_all(dkv.reshape(chips, tokens, -1), 'ctx', 0, 0, axis_index_gr...  26.9 us
    all_to_all x1, blocking collectives, on_device(): all_groups = lax.all_to_all(to_all(kv_grad, groups), 'tp', 0, 0)  14.9 us
    all_to_all x1, waiting for transfers between devices, on_device(): lax.all_to_all(to_all(keys_values, chips), 'ctx', 0, 0, axis_index_groups...  12.3 us
    all_to_all x1, starting transfers between devices, on_device(): lax.all_to_all(to_all(keys_values, chips), 'ctx', 0, 0, axis_index_groups...  9.6 us
    ppermute x4, waiting for transfers between devices, exchanged(): return lax.ppermute(x, 'ctx', other_core)  4.82 us
    all_to_all x1, starting transfers between devices, on_device(): lax.all_to_all(kv_weight.reshape(groups, features, kv_weight.shape[1]), '...  4.51 us
  transfers between devices with their start and end apart: 6, of which 5 were waited for; matrix products, arithmetic and copies ran while one was open for 2% of the time, Pallas kernels for 0%

profile of v1, /device:TPU:32, one launch (start us, length us, event | category | flops | bytes accessed | tf_op | source)
XLA Modules:
  0.0 169.5 jit_solution(11567636008214571172)
XLA Ops:
  0.6 1.7 broadcast_in_dim.4
  2.3 9.6 %all-to-all-start = ((bf16[16,128,128]{2,1,0:T(8,128)(2,1)}), bf16[16,128,128]{2,1,0:T(8,128)(2,1)S(1)}, u32[]{:S(2)}, u32[]{:S(2)}) async-start(bf16[16,128,128]{2,1,0:T(8,128)(2,1)} %broadcast_in_dim.4), calls=%async_computation | async-start | bytes 1048576 | tf_op jit(solution)/shard_map/all_to_all | solution.py:280
  11.9 1.0 constant_dynamic-slice_fusion.2
  12.9 1.1 constant_dynamic-slice_fusion
  14.1 0.1 collective-permute-start.1
  14.2 0.1 reshape.33
  14.4 0.1 reshape.35
  14.5 0.1 reshape.34
  14.6 12.3 %all-to-all-done = bf16[16,128,128]{2,1,0:T(8,128)(2,1)S(1)} async-done(((bf16[16,128,128]{2,1,0:T(8,128)(2,1)}), bf16[16,128,128]{2,1,0:T(8,128)(2,1)S(1)}, u32[]{:S(2)}, u32[]{:S(2)}) %all-to-all-start) | async-done | bytes 524320 | tf_op jit(solution)/shard_map/all_to_all | solution.py:280
  27.1 1.7 %collective-permute-done = bf16[16,128,128]{2,1,0:T(8,128)(2,1)S(1)} collective-permute-done((bf16[16,128,128]{2,1,0:T(8,128)(2,1)S(1)}, bf16[16,128,128]{2,1,0:T(8,128)(2,1)S(1)}, u32[]{:S(2)}, u32[]{:S(2)}) %collective-permute-start) | collective-permute-done | bytes 524320 | tf_op jit(solution)/shard_map/ppermute | solution.py:275
  28.8 36.2 %shard_map.77 = (bf16[128,512]{1,0:T(8,128)(2,1)S(1)}, bf16[128,512]{1,0:T(8,128)(2,1)S(1)}, bf16[32,64,128]{2,1,0:T(8,128)(2,1)S(1)}, bf16[32,64,128]{2,1,0:T(8,128)(2,1)S(1)}) custom-call(s32[64]{0:T(128)S(1)} %pad_add_fusion.slot_pos, s32[4]{0:T(128)S(1)} %pad_add_fusion.1.my_pos, bf16[32,64,128]{2,1,0:T(8,128)(2,1)S(1)} %bitcast.8, ...), custom_call_target="tpu_custom_call" | custom-call | flops 21474836480 | bytes 6291456 | tf_op jit(solution)/shard_map/pallas_call | solution.py:211
  65.0 0.2 collective-permute-start.3
  65.2 1.8 %collective-permute-done.3 = bf16[32,64,128]{2,1,0:T(8,128)(2,1)S(1)} collective-permute-done((bf16[32,64,128]{2,1,0:T(8,128)(2,1)S(1)}, bf16[32,64,128]{2,1,0:T(8,128)(2,1)S(1)}, u32[]{:S(2)}, u32[]{:S(2)}) %collective-permute-start.3) | collective-permute-done | bytes 524320 | tf_op jit(solution)/shard_map/ppermute | solution.py:275
  67.0 0.2 add_convert_fusion
  67.2 26.9 %all_to_all.20 = bf16[16,128,128]{2,1,0:T(8,128)(2,1)S(1)} all-to-all(bf16[16,128,128]{2,1,0:T(8,128)(2,1)S(1)} %bitcast.11), channel_id=1, replica_groups={{0,16,32,48,64,80,96,112,128,144,160,176,192,208,224,240},{8,24,40,56,7..., dimensions={0} | all-to-all | bytes 1048576 | tf_op jit(solution)/shard_map/all_to_all | solution.py:307
  94.1 0.1 reduce_sum.12
  94.2 14.9 %all_to_all.21.kv_ref = bf16[8,128,128]{2,1,0:T(8,128)(2,1)S(1)} all-to-all(bf16[8,128,128]{2,1,0:T(8,128)(2,1)S(1)} %broadcast_in_dim.5), channel_id=1, replica_groups=mesh['ctx'=32,'tp'=8] {'tp'}, dimensions={0} | all-to-all | bytes 524288 | tf_op jit(solution)/shard_map/all_to_all | solution.py:311
  109.1 4.5 %all-to-all-start.3 = ((bf16[8,1856,128]{2,1,0:T(8,128)(2,1)}), bf16[8,1856,128]{2,1,0:T(8,128)(2,1)}, u32[]{:S(2)}, u32[]{:S(2)}) async-start(bf16[8,1856,128]{2,1,0:T(8,128)(2,1)} %bitcast.10), calls=%async_computation.3 | async-start | bytes 7602176 | tf_op jit(solution)/shard_map/all_to_all | solution.py:278
  113.6 0.1 collective-permute-start.2
  113.7 1.3 collective-permute-done.2
  115.0 0.8 maximum_select_fusion
  115.8 49.3 %all-to-all-done.3.w_ref = bf16[8,1856,128]{2,1,0:T(8,128)(2,1)} async-done(((bf16[8,1856,128]{2,1,0:T(8,128)(2,1)}), bf16[8,1856,128]{2,1,0:T(8,128)(2,1)}, u32[]{:S(2)}, u32[]{:S(2)}) %all-to-all-start.3) | async-done | bytes 3801120 | tf_op jit(solution)/shard_map/all_to_all | solution.py:278
  165.1 3.3 %shard_map.78 = bf16[128,1856]{1,0:T(8,128)(2,1)S(1)} custom-call(bf16[8,128,128]{2,1,0:T(8,128)(2,1)S(1)} %all_to_all.21.kv_ref, bf16[8,1856,128]{2,1,0:T(8,128)(2,1)} %all-to-all-done.3.w_ref), custom_call_target="tpu_custom_call" | custom-call | flops 486539264 | bytes 3801088 | tf_op jit(solution)/shard_map/pallas_call | solution.py:248
  168.5 1.0 copy.9
  (11 shorter events, 0.3 us)
Async XLA Ops:
  0.6 13.5 %copy-start = (s32[64]{0:T(128)S(1)}, s32[64]{0:T(128)}, u32[]{:S(2)}) copy-start(s32[64]{0:T(128)} %param.11) | copy-start | bytes 772
  2.3 24.6 %all-to-all-start = ((bf16[16,128,128]{2,1,0:T(8,128)(2,1)}), bf16[16,128,128]{2,1,0:T(8,128)(2,1)S(1)}, u32[]{:S(2)}, u32[]{:S(2)}) async-start(bf16[16,128,128]{2,1,0:T(8,128)(2,1)} %broadcast_in_dim.4), calls=%async_computation | async-start | bytes 1048576 | tf_op jit(solution)/shard_map/all_to_all | solution.py:280
  14.1 13.0 %collective-permute-start.1 = (bf16[128,1536]{1,0:T(8,128)(2,1)S(1)}, bf16[128,1536]{1,0:T(8,128)(2,1)S(1)}, u32[]{:S(2)}, u32[]{:S(2)}) collective-permute-start(bf16[128,1536]{1,0:T(8,128)(2,1)S(1)} %pad_maximum_fusion.1), channel_id=1, source_target_pairs={{0,8},{8,0},{16,24},{24,16},{32,40},{40,32},{48,56},{56,48},{64,72... | collective-permute-start | bytes 1179656 | tf_op jit(solution)/shard_map/ppermute | solution.py:275
  26.9 1.9 %collective-permute-start = (bf16[16,128,128]{2,1,0:T(8,128)(2,1)S(1)}, bf16[16,128,128]{2,1,0:T(8,128)(2,1)S(1)}, u32[]{:S(2)}, u32[]{:S(2)}) collective-permute-start(bf16[16,128,128]{2,1,0:T(8,128)(2,1)S(1)} %all-to-all-done), channel_id=1, source_target_pairs={{0,8},{8,0},{16,24},{24,16},{32,40},{40,32},{48,56},{56,48},{64,72... | collective-permute-start | bytes 1572872 | tf_op jit(solution)/shard_map/ppermute | solution.py:275
  65.0 2.0 %collective-permute-start.3 = (bf16[32,64,128]{2,1,0:T(8,128)(2,1)S(1)}, bf16[32,64,128]{2,1,0:T(8,128)(2,1)S(1)}, u32[]{:S(2)}, u32[]{:S(2)}) collective-permute-start(bf16[32,64,128]{2,1,0:T(8,128)(2,1)S(1)} %get-tuple-element.9), channel_id=1, source_target_pairs={{0,8},{8,0},{16,24},{24,16},{32,40},{40,32},{48,56},{56,48},{64,72... | collective-permute-start | bytes 1572872 | tf_op jit(solution)/shard_map/ppermute | solution.py:275
  109.1 56.1 %all-to-all-start.3 = ((bf16[8,1856,128]{2,1,0:T(8,128)(2,1)}), bf16[8,1856,128]{2,1,0:T(8,128)(2,1)}, u32[]{:S(2)}, u32[]{:S(2)}) async-start(bf16[8,1856,128]{2,1,0:T(8,128)(2,1)} %bitcast.10), calls=%async_computation.3 | async-start | bytes 7602176 | tf_op jit(solution)/shard_map/all_to_all | solution.py:278
  113.6 1.4 collective-permute-start.2

commit v2 on v1

v2 whole, which is shorter than its diff:
```python
import functools

import jax
import jax.numpy as jnp
from jax import lax
from jax.experimental import pallas as pl
from jax.experimental.pallas import tpu as pltpu
from jax.sharding import PartitionSpec as P

HEAD = 64
SPAN = 64
BLOCK = 512
PAIR = 2 * HEAD
SCALE = 0.125
LOG2E = 1.4426950408889634
MASKED = -1e30

f32 = jnp.float32
bf16 = jnp.bfloat16


def dot_t(a, b):
    return lax.dot_general(a, b, (((1,), (1,)), ((), ())), preferred_element_type=f32)


def dot(a, b):
    return lax.dot_general(a, b, (((1,), (0,)), ((), ())), preferred_element_type=f32)


def swap_halves(x):
    return pltpu.roll(x.astype(f32), HEAD, 1)


def prepare_kernel(rows_a, rows_b, mixed, plain):
    spans = rows_a.shape[0] // SPAN
    width = rows_a.shape[1] // 3
    pairs = width // PAIR
    qcount = pairs * SPAN
    line = lax.broadcasted_iota(jnp.int32, (HEAD, qcount), 0)

    def parts(d):
        a = d.astype(bf16).astype(f32)
        b = (d - a).astype(bf16).astype(f32)
        c = d - a - b
        return jnp.where(line == 0, a, jnp.where(line == 1, b, jnp.where(line == 2, c, 0.0)))

    for which, rows in enumerate((rows_a, rows_b)):
        for i in range(spans):
            n = which * spans + i

            def turned(part):
                stack = jnp.concatenate(
                    [
                        rows[i * SPAN : (i + 1) * SPAN, part * width + p * PAIR : part * width + (p + 1) * PAIR]
                        for p in range(pairs)
                    ],
                    axis=0,
                )
                return jnp.transpose(stack.astype(f32))

            q = turned(0)
            do = turned(1)
            prod = do * turned(2)
            q2 = q * (SCALE * LOG2E)
            hi = q2.astype(bf16).astype(f32)
            lo = q2 - hi
            for e in range(2):
                part = slice(e * HEAD, (e + 1) * HEAD)
                cols = slice(e * qcount, (e + 1) * qcount)
                mixed[n, 0, 0:HEAD, cols] = hi[part].astype(bf16)
                mixed[n, 0, HEAD:PAIR, cols] = lo[part].astype(bf16)
                mixed[n, 1, 0:HEAD, cols] = do[part].astype(bf16)
                mixed[n, 1, HEAD:PAIR, cols] = parts(-jnp.sum(prod[part], axis=0, keepdims=True)).astype(bf16)
                plain[n, :, cols] = q[part].astype(bf16)


def prepared_rows(rows_a, rows_b):
    spans = 2 * rows_a.shape[0] // SPAN
    qcount = rows_a.shape[1] // 3 // PAIR * SPAN
    vmem = pl.BlockSpec(memory_space=pltpu.VMEM)
    return pl.pallas_call(
        prepare_kernel,
        out_shape=(
            jax.ShapeDtypeStruct((spans, 2, PAIR, 2 * qcount), bf16),
            jax.ShapeDtypeStruct((spans, HEAD, 2 * qcount), bf16),
        ),
        in_specs=[vmem, vmem],
        out_specs=(vmem, vmem),
        compiler_params=pltpu.CompilerParams(vmem_limit_bytes=16 * 1024 * 1024),
        cost_estimate=pl.CostEstimate(flops=1 << 24, bytes_accessed=3 << 20, transcendentals=0),
    )(rows_a, rows_b)


def attention_kernel(
    slot_pos,
    my_pos,
    kv_a,
    kv_b,
    mixed,
    plain,
    dq,
    dkv_a,
    dkv_b,
    kv_sorted,
    kk,
    va,
    kt,
    scores_0,
    scores_1,
    weights_0,
    weights_1,
    dscores_0,
    dscores_1,
    acc,
    dqt,
):
    scores = (scores_0, scores_1)
    weights = (weights_0, weights_1)
    dscores = (dscores_0, dscores_1)
    half_slots = kv_a.shape[0]
    blocks = kk.shape[0]
    per_block = BLOCK // SPAN
    qcount = plain.shape[2] // 2
    pairs = qcount // SPAN

    def place(slot, _):
        for which, src in enumerate((kv_a, kv_b)):
            p = slot_pos[which * half_slots + slot]
            row = pl.multiple_of((p % per_block) * SPAN, SPAN)
            kv_sorted[p // per_block, pl.ds(row, SPAN), :] = src[slot]
        return 0

    lax.fori_loop(0, half_slots, place, 0, unroll=8)

    lane_k = lax.broadcasted_iota(jnp.int32, (BLOCK, PAIR), 1)
    low_k = lane_k < HEAD
    ones_hi = ((lane_k >= HEAD) & (lane_k < HEAD + 3)).astype(f32)

    def prepare(b, _):
        kv = kv_sorted[b].astype(f32)
        vk = pltpu.roll(kv, HEAD, 1)
        kk[b] = jnp.where(low_k, kv, vk).astype(bf16)
        va[b] = jnp.where(low_k, vk, ones_hi).astype(bf16)
        kt[b] = jnp.transpose(kv)[:HEAD].astype(bf16)
        acc[b] = jnp.zeros((PAIR, BLOCK), f32)
        return 0

    lax.fori_loop(0, blocks, prepare, 0)

    key_row = lax.broadcasted_iota(jnp.int32, (BLOCK, 2 * qcount), 0)
    query_row = lax.broadcasted_iota(jnp.int32, (BLOCK, 2 * qcount), 1) % SPAN

    def one_span(n, _):
        pos = my_pos[n]
        last = pos // per_block

        def block_of(u):
            return jnp.where(u == 0, last, u - 1)

        def products(u, parity, masked=False):
            s = dot(kk[block_of(u)], mixed[n, 0])
            if masked:
                s = jnp.where(key_row <= (pos % per_block) * SPAN + query_row, s, MASKED)
            scores[parity][u // 2] = s
            return jnp.max(s, axis=0, keepdims=True)

        def summed(u, parity, top):
            return jnp.sum(jnp.exp2(scores[parity][u // 2] - top), axis=0, keepdims=True)

        def stats(u, parity, running):
            top, l = running
            higher = jnp.maximum(top, products(u, parity))
            l = l + summed(u - 1, 1 - parity, top)
            return higher, l * jnp.exp2(top - higher)

        def terms(u, parity):
            p = jnp.exp2(scores[parity][u // 2] - lse)
            ds = p * dot(va[block_of(u)], mixed[n, 1])
            weights[parity][...] = p.astype(bf16)
            dscores[parity][...] = ds.astype(bf16)

        def sums(u, parity):
            b = block_of(u)
            ds = dscores[parity][...]
            dqt[...] += dot(kt[b], ds)
            acc[b, 0:HEAD] += dot_t(plain[n], ds)
            acc[b, HEAD:PAIR] += dot_t(mixed[n, 1, 0:HEAD], weights[parity][...])

        def both(t, running):
            running = stats(2 * t + 1, 1, running)
            return stats(2 * t + 2, 0, running)

        pairs_left = last // 2
        odd = last % 2 == 1
        running = (products(0, 0, True), jnp.zeros((1, 2 * qcount), f32))
        running = lax.fori_loop(0, pairs_left, both, running)

        def with_odd(running):
            top, l = stats(last, 1, running)
            return top, l + summed(last, 1, top)

        def without(running):
            top, l = running
            return top, l + summed(last, 0, top)

        top, l = lax.cond(odd, with_odd, without, running)
        lse = top + jnp.log2(l)

        dqt[...] = jnp.zeros_like(dqt)
        terms(0, 0)

        def grads(t, _):
            sums(2 * t, 0)
            terms(2 * t + 1, 1)
            sums(2 * t + 1, 1)
            terms(2 * t + 2, 0)
            return 0

        lax.fori_loop(0, pairs_left, grads, 0)

        @pl.when(odd)
        def _():
            sums(last - 1, 0)
            terms(last, 1)
            sums(last, 1)

        @pl.when(jnp.logical_not(odd))
        def _():
            sums(last, 0)

        total = jnp.concatenate([dqt[:, :qcount], dqt[:, qcount:]], axis=0)
        total = (jnp.transpose(total) * SCALE).astype(bf16)
        row = pl.multiple_of(n * SPAN, SPAN)
        for p in range(pairs):
            dq[pl.ds(row, SPAN), p * PAIR : (p + 1) * PAIR] = total[p * SPAN : (p + 1) * SPAN]
        return 0

    lax.fori_loop(0, plain.shape[0], one_span, 0)

    line = lax.broadcasted_iota(jnp.int32, (PAIR, BLOCK), 0)
    factor = jnp.where(line < HEAD, SCALE, 1.0)

    def finish(b, _):
        kv_sorted[b] = jnp.transpose(acc[b] * factor).astype(bf16)
        return 0

    lax.fori_loop(0, blocks, finish, 0)

    def collect(slot, _):
        for which, dst in enumerate((dkv_a, dkv_b)):
            p = slot_pos[which * half_slots + slot]
            row = pl.multiple_of((p % per_block) * SPAN, SPAN)
            dst[slot] = kv_sorted[p // per_block, pl.ds(row, SPAN), :]
        return 0

    lax.fori_loop(0, half_slots, collect, 0, unroll=8)


def attention_grads(slot_pos, my_pos, kv_a, kv_b, prepared):
    mixed, plain = prepared
    slots = 2 * kv_a.shape[0]
    blocks = slots * SPAN // BLOCK
    half_blocks = (blocks + 1) // 2
    spans = plain.shape[0]
    qcount = plain.shape[2] // 2
    pairs = qcount // SPAN
    smem = pl.BlockSpec(memory_space=pltpu.SMEM)
    vmem = pl.BlockSpec(memory_space=pltpu.VMEM)
    terms = slots * SPAN * spans * qcount * 2
    return pl.pallas_call(
        attention_kernel,
        out_shape=(
            jax.ShapeDtypeStruct((spans * SPAN, pairs * PAIR), bf16),
            jax.ShapeDtypeStruct(kv_a.shape, bf16),
            jax.ShapeDtypeStruct(kv_b.shape, bf16),
        ),
        in_specs=[smem, smem, vmem, vmem, vmem, vmem],
        out_specs=(vmem, vmem, vmem),
        scratch_shapes=[
            pltpu.VMEM((blocks, BLOCK, PAIR), bf16),
            pltpu.VMEM((blocks, BLOCK, PAIR), bf16),
            pltpu.VMEM((blocks, BLOCK, PAIR), bf16),
            pltpu.VMEM((blocks, HEAD, BLOCK), bf16),
            pltpu.VMEM((half_blocks, BLOCK, 2 * qcount), f32),
            pltpu.VMEM((half_blocks, BLOCK, 2 * qcount), f32),
            pltpu.VMEM((BLOCK, 2 * qcount), bf16),
            pltpu.VMEM((BLOCK, 2 * qcount), bf16),
            pltpu.VMEM((BLOCK, 2 * qcount), bf16),
            pltpu.VMEM((BLOCK, 2 * qcount), bf16),
            pltpu.VMEM((blocks, PAIR, BLOCK), f32),
            pltpu.VMEM((HEAD, 2 * qcount), f32),
        ],
        compiler_params=pltpu.CompilerParams(vmem_limit_bytes=48 * 1024 * 1024),
        cost_estimate=pl.CostEstimate(flops=terms * HEAD * 2 * 5 * 4, bytes_accessed=6 << 20, transcendentals=terms),
    )(slot_pos, my_pos, kv_a, kv_b, mixed, plain)


def project_kernel(core, kv, w_mine, w_other, out):
    rows = w_mine.shape[1]
    for w, part in ((w_mine, core[0]), (w_other, 1 - core[0])):
        total = dot_t(w[0], kv[0])
        for g in range(1, kv.shape[0]):
            total = total + dot_t(w[g], kv[g])
        out[pl.ds(pl.multiple_of(part * rows, 16), rows), :] = total.astype(bf16)


def project(core, kv, w_mine, w_other):
    smem = pl.BlockSpec(memory_space=pltpu.SMEM)
    vmem = pl.BlockSpec(memory_space=pltpu.VMEM)
    return pl.pallas_call(
        project_kernel,
        out_shape=jax.ShapeDtypeStruct((2 * w_mine.shape[1], kv.shape[1]), bf16),
        in_specs=[smem, vmem, vmem, vmem],
        out_specs=vmem,
        compiler_params=pltpu.CompilerParams(vmem_limit_bytes=24 * 1024 * 1024),
        cost_estimate=pl.CostEstimate(
            flops=4 * kv.size * w_mine.shape[1], bytes_accessed=4 * w_mine.size, transcendentals=0
        ),
    )(core[None], kv, w_mine, w_other).T


def on_device(queries, keys_values, forward_out, out_grad, kv_weight, span_table):
    tokens = queries.shape[0]
    half = queries.shape[1] // 2
    me = lax.axis_index("ctx")
    core = me % 2
    chip = me // 2
    count = lax.axis_size("ctx")
    groups = lax.axis_size("tp")
    chips = count // 2
    same_core = [[2 * c + k for c in range(chips)] for k in range(2)]
    other_core = [(i, i ^ 1) for i in range(count)]

    def to_all(x, n):
        return jnp.broadcast_to(x[None], (n,) + x.shape)

    def exchanged(x):
        return lax.ppermute(x, "ctx", other_core)

    kv_a = lax.all_to_all(to_all(keys_values, chips), "ctx", 0, 0, axis_index_groups=same_core)

    features = kv_weight.shape[0] // groups
    w_part = lax.dynamic_index_in_dim(
        kv_weight.reshape(groups, 2, features // 2, kv_weight.shape[1]), core, 1, False
    )
    kv_a, w_part = lax.optimization_barrier((kv_a, w_part))
    w_mine = lax.all_to_all(w_part, "tp", 0, 0)
    kv_b = exchanged(kv_a)

    def my_heads(k):
        return [lax.dynamic_slice_in_dim(x, k * half, half, 1) for x in (queries, out_grad, forward_out)]

    rows_a = jnp.concatenate(my_heads(core), axis=1)
    rows_b = exchanged(jnp.concatenate(my_heads(1 - core), axis=1))

    spans = tokens // SPAN
    by_device = span_table.reshape(chips, 2, spans)
    mine = lax.dynamic_index_in_dim(by_device, core, 1, False)
    theirs = lax.dynamic_index_in_dim(by_device, 1 - core, 1, False)
    slot_pos = jnp.concatenate([mine.reshape(-1), theirs.reshape(-1)])
    my_pos = jnp.concatenate(
        [
            lax.dynamic_index_in_dim(mine, chip, 0, False),
            lax.dynamic_index_in_dim(theirs, chip, 0, False),
        ]
    )

    by_span = (chips * spans, SPAN, keys_values.shape[1])
    prepared = prepared_rows(rows_a, rows_b)
    dq, dkv_a, dkv_b = attention_grads(
        slot_pos, my_pos, kv_a.reshape(by_span), kv_b.reshape(by_span), prepared
    )
    dkv_b, w_mine = lax.optimization_barrier((dkv_b, w_mine))
    dkv = (dkv_a.astype(f32) + exchanged(dkv_b).astype(f32)).astype(bf16)
    w_other = exchanged(w_mine)
    terms = lax.all_to_all(
        dkv.reshape(chips, tokens, -1), "ctx", 0, 0, axis_index_groups=same_core
    )
    kv_grad = jnp.sum(terms.astype(f32), axis=0).astype(bf16)
    all_groups = lax.all_to_all(to_all(kv_grad, groups), "tp", 0, 0)
    input_grad = project(core, all_groups, w_mine, w_other)
    dq_a = dq[:tokens]
    dq_b = exchanged(dq[tokens:])
    query_grad = jnp.where(
        core == 0,
        jnp.concatenate([dq_a, dq_b], axis=1),
        jnp.concatenate([dq_b, dq_a], axis=1),
    )
    return query_grad, input_grad


def solution(mesh):
    placed = (P("ctx", "tp"), P("ctx", "tp"), P("ctx", "tp"), P("ctx", "tp"), P(None, "tp"), P())
    return jax.shard_map(
        on_device,
        mesh=mesh,
        in_specs=placed,
        out_specs=(P("ctx", "tp"), P("ctx", "tp")),
        check_vma=False,
    )
```

time: 169 us -> 113 us (0.67)
  blocking collectives: 41.8 us -> 0 us
  waiting for transfers between devices: 66.4 us -> 38.1 us
  starting transfers between devices: 14.5 us -> 32 us
  Pallas kernels: 39.5 us -> 27.2 us
  local copies, waits for them, and re-layouts: 5.15 us -> 11.6 us
    all_to_all x2 -> x0, blocking collectives: 41.8 us -> none  [the longest x1 26.9 us: on_device(): lax.all_to_all(dkv.reshape(chips, tokens, -1), 'ctx', 0, 0, axis_index_gr...]
    all_to_all x1 -> x3, waiting for transfers between devices: 49.3 us -> 25.4 us  [the longest x1 15.6 us: on_device(): lax.all_to_all(dkv.reshape(chips, tokens, -1), 'ctx', 0, 0, axis_index_gr...]
    all_to_all x1 -> x3, starting transfers between devices: 4.51 us -> 21.7 us  [the longest x1 7.79 us: on_device(): all_groups = lax.all_to_all(to_all(kv_grad, groups), 'tp', 0, 0)]
    pallas_call x2 -> x3, Pallas kernels: 39.5 us -> 27.2 us  [the longest x1 23.5 us: attention_grads(): pl.pallas_call(attention_kernel, out_shape=(jax.ShapeDtypeStruct((spans *...]
    unnamed x3 -> x16, local copies, waits for them, and re-layouts: 0.99 us -> 4.83 us
    squeeze x0 -> x1, local copies, waits for them, and re-layouts: none -> 2.95 us  [on_device(): lax.dynamic_index_in_dim(kv_weight.reshape(groups, 2, features // 2, kv_w...]
    ppermute x4 -> x5, waiting for transfers between devices: 4.82 us -> 2.33 us  [exchanged(): return lax.ppermute(x, 'ctx', other_core)]
    all_to_all x1, waiting for transfers between devices: 12.3 us -> 10.4 us  [on_device(): lax.all_to_all(to_all(keys_values, chips), 'ctx', 0, 0, axis_index_groups...]
  transfers between devices with their start and end apart: 6 -> 9, of which waited for: 5 -> 5; matrix products, arithmetic and copies ran while one was open for 2% -> 6% of each run, Pallas kernels for 0% -> 21%
where the time goes in v2:
time: 113 us; the launch traced here: 112 us
  waiting for transfers between devices  38.1 us (34%)
  starting transfers between devices  32 us (28%)
  Pallas kernels  27.2 us (24%)
  local copies, waits for them, and re-layouts  11.6 us (10%)
  other arithmetic  2.06 us (2%)
    pallas_call x1, Pallas kernels, attention_grads(): pl.pallas_call(attention_kernel, out_shape=(jax.ShapeDtypeStruct((spans *...  23.5 us
    all_to_all x1, waiting for transfers between devices, on_device(): lax.all_to_all(dkv.reshape(chips, tokens, -1), 'ctx', 0, 0, axis_index_gr...  15.6 us
    all_to_all x1, waiting for transfers between devices, on_device(): lax.all_to_all(to_all(keys_values, chips), 'ctx', 0, 0, axis_index_groups...  10.4 us
    all_to_all x1, starting transfers between devices, on_device(): lax.all_to_all(to_all(keys_values, chips), 'ctx', 0, 0, axis_index_groups...  9.6 us
    all_to_all x1, starting transfers between devices, on_device(): all_groups = lax.all_to_all(to_all(kv_grad, groups), 'tp', 0, 0)  7.79 us
    all_to_all x1, waiting for transfers between devices, on_device(): all_groups = lax.all_to_all(to_all(kv_grad, groups), 'tp', 0, 0)  7.64 us
    all_to_all x1, starting transfers between devices, on_device(): lax.all_to_all(dkv.reshape(chips, tokens, -1), 'ctx', 0, 0, axis_index_gr...  7.27 us
    all_to_all x1, starting transfers between devices, on_device(): w_mine = lax.all_to_all(w_part, 'tp', 0, 0)  6.64 us
  transfers between devices with their start and end apart: 9, of which 5 were waited for; matrix products, arithmetic and copies ran while one was open for 6% of the time, Pallas kernels for 21%

profile of v2, /device:TPU:32, one launch (start us, length us, event | category | flops | bytes accessed | tf_op | source)
XLA Modules:
  0.0 111.9 jit_solution(17878722180642169697)
XLA Ops:
  0.7 1.7 %broadcast_in_dim.6 = bf16[16,128,128]{2,1,0:T(8,128)(2,1)} broadcast(bf16[128,128]{1,0:T(8,128)(2,1)} %param.7), dimensions={1,2} | broadcast | bytes 557056 | tf_op jit(solution)/shard_map/broadcast_in_dim | solution.py:335
  2.4 9.6 %all-to-all-start = ((bf16[16,128,128]{2,1,0:T(8,128)(2,1)}), bf16[16,128,128]{2,1,0:T(8,128)(2,1)S(1)}, u32[]{:S(2)}, u32[]{:S(2)}) async-start(bf16[16,128,128]{2,1,0:T(8,128)(2,1)} %broadcast_in_dim.6), calls=%async_computation | async-start | bytes 1048576 | tf_op jit(solution)/shard_map/all_to_all | solution.py:340
  12.0 1.0 constant_dynamic-slice_fusion.2
  13.6 2.9 %dynamic-slice_bitcast_fusion = bf16[8,928,128]{2,1,0:T(8,128)(2,1)} fusion(bf16[8,2,928,128]{3,2,1,0:T(8,128)(2,1)} %bitcast.16, s32[]{:T(128)S(6)} %select_n.51), kind=kLoop, calls=%fused_computation | loop fusion | bytes 3801092 | tf_op jit(solution)/shard_map/jit(dynamic_index_in_dim)/squeeze | solution.py:343
  16.5 10.4 %all-to-all-done = bf16[16,128,128]{2,1,0:T(8,128)(2,1)S(1)} async-done(((bf16[16,128,128]{2,1,0:T(8,128)(2,1)}), bf16[16,128,128]{2,1,0:T(8,128)(2,1)S(1)}, u32[]{:S(2)}, u32[]{:S(2)}) %all-to-all-start) | async-done | bytes 524320 | tf_op jit(solution)/shard_map/all_to_all | solution.py:340
  27.2 0.3 shard_map.77
  27.5 1.0 copy-done
  28.5 6.6 %all-to-all-start.1 = ((bf16[8,928,128]{2,1,0:T(8,128)(2,1)}), bf16[8,928,128]{2,1,0:T(8,128)(2,1)S(1)}, u32[]{:S(2)}, u32[]{:S(2)}) async-start(bf16[8,928,128]{2,1,0:T(8,128)(2,1)} %dynamic-slice_bitcast_fusion), calls=%async_computation.1 | async-start | bytes 3801088 | tf_op jit(solution)/shard_map/all_to_all | solution.py:347
  35.1 0.8 copy-done.2
  35.9 1.2 %copy-done.1 = bf16[4,2,128,512]{3,2,1,0:T(8,128)(2,1)S(1)} copy-done((bf16[4,2,128,512]{3,2,1,0:T(8,128)(2,1)S(1)}, bf16[4,2,128,512]{3,2,1,0:T(8,128)(2,1)}, u32[]{:S(2)}) %copy-start.1) | copy-done | bytes 1048600
  37.1 1.0 copy-done.3
  38.2 23.5 %shard_map.78 = (bf16[256,512]{1,0:T(8,128)(2,1)S(1)}, bf16[32,64,128]{2,1,0:T(8,128)(2,1)S(1)}, bf16[32,64,128]{2,1,0:T(8,128)(2,1)S(1)}) custom-call(s32[64]{0:T(128)S(1)} %pad_add_fusion.slot_pos, s32[4]{0:T(128)S(1)} %pad_add_fusion.1.my_pos, bf16[32,64,128]{2,1,0:T(8,128)(2,1)S(1)} %bitcast.14, bf16[32,64,128]{2,1,0:T(8,128)(2,1)S(1)} %bitcast.15, ...), custom_call_target="tpu_custom_call" | custom-call | flops 21474836480 | bytes 6291456 | tf_op jit(solution)/shard_map/pallas_call | solution.py:270
  61.7 0.8 copy-done.4
  62.5 2.1 %all-to-all-done.1.w_mine = bf16[8,928,128]{2,1,0:T(8,128)(2,1)S(1)} async-done(((bf16[8,928,128]{2,1,0:T(8,128)(2,1)}), bf16[8,928,128]{2,1,0:T(8,128)(2,1)S(1)}, u32[]{:S(2)}, u32[]{:S(2)}) %all-to-all-start.1) | async-done | bytes 1900576 | tf_op jit(solution)/shard_map/all_to_all | solution.py:347
  64.6 0.5 collective-permute-start.4
  65.1 2.3 %collective-permute-done.3 = bf16[32,64,128]{2,1,0:T(8,128)(2,1)S(1)} collective-permute-done((bf16[32,64,128]{2,1,0:T(8,128)(2,1)}, bf16[32,64,128]{2,1,0:T(8,128)(2,1)S(1)}, u32[]{:S(2)}, u32[]{:S(2)}) %collective-permute-start.3) | collective-permute-done | bytes 524320 | tf_op jit(solution)/shard_map/ppermute | solution.py:338
  67.4 1.0 add_convert_fusion
  68.4 7.3 %all-to-all-start.2 = ((bf16[16,128,128]{2,1,0:T(8,128)(2,1)}), bf16[16,128,128]{2,1,0:T(8,128)(2,1)S(1)}, u32[]{:S(2)}, u32[]{:S(2)}) async-start(bf16[16,128,128]{2,1,0:T(8,128)(2,1)} %bitcast.7), calls=%async_computation.2 | async-start | bytes 1048576 | tf_op jit(solution)/shard_map/all_to_all | solution.py:376
  75.8 15.6 %all-to-all-done.2 = bf16[16,128,128]{2,1,0:T(8,128)(2,1)S(1)} async-done(((bf16[16,128,128]{2,1,0:T(8,128)(2,1)}), bf16[16,128,128]{2,1,0:T(8,128)(2,1)S(1)}, u32[]{:S(2)}, u32[]{:S(2)}) %all-to-all-start.2) | async-done | bytes 524320 | tf_op jit(solution)/shard_map/all_to_all | solution.py:376
  91.5 0.7 broadcast_in_dim.8
  92.2 7.8 %all-to-all-start.3 = ((bf16[8,128,128]{2,1,0:T(8,128)(2,1)}), bf16[8,128,128]{2,1,0:T(8,128)(2,1)S(1)}, u32[]{:S(2)}, u32[]{:S(2)}) async-start(bf16[8,128,128]{2,1,0:T(8,128)(2,1)} %broadcast_in_dim.8), calls=%async_computation.3 | async-start | bytes 524288 | tf_op jit(solution)/shard_map/all_to_all | solution.py:380
  100.0 0.8 maximum_select_fusion
  100.8 7.6 %all-to-all-done.3.kv = bf16[8,128,128]{2,1,0:T(8,128)(2,1)S(1)} async-done(((bf16[8,128,128]{2,1,0:T(8,128)(2,1)}), bf16[8,128,128]{2,1,0:T(8,128)(2,1)S(1)}, u32[]{:S(2)}, u32[]{:S(2)}) %all-to-all-start.3) | async-done | bytes 262176 | tf_op jit(solution)/shard_map/all_to_all | solution.py:380
  108.5 3.4 %shard_map.79 = bf16[1856,128]{1,0:T(8,128)(2,1)} custom-call(s32[1]{0:T(128)} %bitcast.6.core, bf16[8,128,128]{2,1,0:T(8,128)(2,1)S(1)} %all-to-all-done.3.kv, bf16[8,928,128]{2,1,0:T(8,128)(2,1)S(1)} %all-to-all-done.1.w_mine, bf16[8,928,128]{2,1,0:T(8,128)(2,1)} %collective-permute-done.4.w_other), custom_call_target="tpu_custom_call" | custom-call | flops 486539264 | bytes 3801088 | tf_op jit(solution)/shard_map/pallas_call | solution.py:310
  (31 shorter events, 0.9 us)
Async XLA Ops:
  0.6 12.3 %copy-start.5 = (bf16[128,1024]{1,0:T(8,128)(2,1)S(1)}, bf16[128,1024]{1,0:T(8,128)(2,1)}, u32[]{:S(2)}) copy-start(bf16[128,1024]{1,0:T(8,128)(2,1)} %param.8) | copy-start | bytes 786436
  0.6 12.3 %copy-start.6 = (bf16[128,1024]{1,0:T(8,128)(2,1)S(1)}, bf16[128,1024]{1,0:T(8,128)(2,1)}, u32[]{:S(2)}) copy-start(bf16[128,1024]{1,0:T(8,128)(2,1)} %param.9) | copy-start | bytes 786436
  0.7 12.5 %copy-start.7 = (s32[64]{0:T(128)S(1)}, s32[64]{0:T(128)}, u32[]{:S(2)}) copy-start(s32[64]{0:T(128)} %param.11) | copy-start | bytes 772
  2.4 24.6 %all-to-all-start = ((bf16[16,128,128]{2,1,0:T(8,128)(2,1)}), bf16[16,128,128]{2,1,0:T(8,128)(2,1)S(1)}, u32[]{:S(2)}, u32[]{:S(2)}) async-start(bf16[16,128,128]{2,1,0:T(8,128)(2,1)} %broadcast_in_dim.6), calls=%async_computation | async-start | bytes 1048576 | tf_op jit(solution)/shard_map/all_to_all | solution.py:340
  13.1 14.1 %collective-permute-start.1 = (bf16[128,1536]{1,0:T(8,128)(2,1)S(1)}, bf16[128,1536]{1,0:T(8,128)(2,1)S(1)}, u32[]{:S(2)}, u32[]{:S(2)}) collective-permute-start(bf16[128,1536]{1,0:T(8,128)(2,1)S(1)} %pad_maximum_fusion.1), channel_id=1, source_target_pairs={{0,8},{8,0},{16,24},{24,16},{32,40},{40,32},{48,56},{56,48},{64,72... | collective-permute-start | bytes 1179656 | tf_op jit(solution)/shard_map/ppermute | solution.py:338
  27.0 8.2 %collective-permute-start = (bf16[16,128,128]{2,1,0:T(8,128)(2,1)S(1)}, bf16[16,128,128]{2,1,0:T(8,128)(2,1)S(1)}, u32[]{:S(2)}, u32[]{:S(2)}) collective-permute-start(bf16[16,128,128]{2,1,0:T(8,128)(2,1)S(1)} %all-to-all-done), channel_id=1, source_target_pairs={{0,8},{8,0},{16,24},{24,16},{32,40},{40,32},{48,56},{56,48},{64,72... | collective-permute-start | bytes 1572872 | tf_op jit(solution)/shard_map/ppermute | solution.py:338
  27.5 1.0 copy-start
  28.5 36.1 %all-to-all-start.1 = ((bf16[8,928,128]{2,1,0:T(8,128)(2,1)}), bf16[8,928,128]{2,1,0:T(8,128)(2,1)S(1)}, u32[]{:S(2)}, u32[]{:S(2)}) async-start(bf16[8,928,128]{2,1,0:T(8,128)(2,1)} %dynamic-slice_bitcast_fusion), calls=%async_computation.1 | async-start | bytes 3801088 | tf_op jit(solution)/shard_map/all_to_all | solution.py:347
  35.1 0.8 copy-start.2
  35.9 1.2 %copy-start.1 = (bf16[4,2,128,512]{3,2,1,0:T(8,128)(2,1)S(1)}, bf16[4,2,128,512]{3,2,1,0:T(8,128)(2,1)}, u32[]{:S(2)}) copy-start(bf16[4,2,128,512]{3,2,1,0:T(8,128)(2,1)} %copy-done) | copy-start | bytes 3145732
  37.1 1.0 copy-start.3
  61.7 0.8 copy-start.4
  64.6 2.8 %collective-permute-start.3 = (bf16[32,64,128]{2,1,0:T(8,128)(2,1)}, bf16[32,64,128]{2,1,0:T(8,128)(2,1)S(1)}, u32[]{:S(2)}, u32[]{:S(2)}) collective-permute-start(bf16[32,64,128]{2,1,0:T(8,128)(2,1)} %copy-done.4), channel_id=1, source_target_pairs={{0,8},{8,0},{16,24},{24,16},{32,40},{40,32},{48,56},{56,48},{64,72... | collective-permute-start | bytes 1572872 | tf_op jit(solution)/shard_map/ppermute | solution.py:338
  64.6 43.9 %collective-permute-start.4 = (bf16[8,928,128]{2,1,0:T(8,128)(2,1)S(1)}, bf16[8,928,128]{2,1,0:T(8,128)(2,1)}, u32[]{:S(2)}, u32[]{:S(2)}) collective-permute-start(bf16[8,928,128]{2,1,0:T(8,128)(2,1)S(1)} %all-to-all-done.1.w_mine), channel_id=1, source_target_pairs={{0,8},{8,0},{16,24},{24,16},{32,40},{40,32},{48,56},{56,48},{64,72... | collective-permute-start | bytes 5701640 | tf_op jit(solution)/shard_map/ppermute | solution.py:338
  68.4 23.0 %all-to-all-start.2 = ((bf16[16,128,128]{2,1,0:T(8,128)(2,1)}), bf16[16,128,128]{2,1,0:T(8,128)(2,1)S(1)}, u32[]{:S(2)}, u32[]{:S(2)}) async-start(bf16[16,128,128]{2,1,0:T(8,128)(2,1)} %bitcast.7), calls=%async_computation.2 | async-start | bytes 1048576 | tf_op jit(solution)/shard_map/all_to_all | solution.py:376
  75.7 24.3 %collective-permute-start.2 = (bf16[128,512]{1,0:T(8,128)(2,1)S(1)}, bf16[128,512]{1,0:T(8,128)(2,1)S(1)}, u32[]{:S(2)}, u32[]{:S(2)}) collective-permute-start(bf16[128,512]{1,0:T(8,128)(2,1)S(1)} %get-tuple-element.23), channel_id=1, source_target_pairs={{0,8},{8,0},{16,24},{24,16},{32,40},{40,32},{48,56},{56,48},{64,72... | collective-permute-start | bytes 393224 | tf_op jit(solution)/shard_map/ppermute | solution.py:338
  92.2 16.2 %all-to-all-start.3 = ((bf16[8,128,128]{2,1,0:T(8,128)(2,1)}), bf16[8,128,128]{2,1,0:T(8,128)(2,1)S(1)}, u32[]{:S(2)}, u32[]{:S(2)}) async-start(bf16[8,128,128]{2,1,0:T(8,128)(2,1)} %broadcast_in_dim.8), calls=%async_computation.3 | async-start | bytes 524288 | tf_op jit(solution)/shard_map/all_to_all | solution.py:380

commit v3 on v2

--- a/solution.py
+++ b/solution.py
@@ -86,7 +86,7 @@
         ),
         in_specs=[vmem, vmem],
         out_specs=(vmem, vmem),
-        compiler_params=pltpu.CompilerParams(vmem_limit_bytes=16 * 1024 * 1024),
+        compiler_params=pltpu.CompilerParams(vmem_limit_bytes=8 * 1024 * 1024),
         cost_estimate=pl.CostEstimate(flops=1 << 24, bytes_accessed=3 << 20, transcendentals=0),
     )(rows_a, rows_b)
 
@@ -107,15 +107,16 @@
     kt,
     scores_0,
     scores_1,
-    weights_0,
-    weights_1,
+    held_0,
+    held_1,
     dscores_0,
     dscores_1,
+    tops,
     acc,
     dqt,
 ):
     scores = (scores_0, scores_1)
-    weights = (weights_0, weights_1)
+    held = (held_0, held_1)
     dscores = (dscores_0, dscores_1)
     half_slots = kv_a.shape[0]
     blocks = kk.shape[0]
@@ -145,7 +146,7 @@
         acc[b] = jnp.zeros((PAIR, BLOCK), f32)
         return 0
 
-    lax.fori_loop(0, blocks, prepare, 0)
+    lax.fori_loop(0, blocks, prepare, 0, unroll=4)
 
     key_row = lax.broadcasted_iota(jnp.int32, (BLOCK, 2 * qcount), 0)
     query_row = lax.broadcasted_iota(jnp.int32, (BLOCK, 2 * qcount), 1) % SPAN
@@ -157,77 +158,87 @@
         def block_of(u):
             return jnp.where(u == 0, last, u - 1)
 
-        def products(u, parity, masked=False):
+        def first(u, parity, top, masked=False):
             s = dot(kk[block_of(u)], mixed[n, 0])
             if masked:
                 s = jnp.where(key_row <= (pos % per_block) * SPAN + query_row, s, MASKED)
-            scores[parity][u // 2] = s
-            return jnp.max(s, axis=0, keepdims=True)
-
-        def summed(u, parity, top):
-            return jnp.sum(jnp.exp2(scores[parity][u // 2] - top), axis=0, keepdims=True)
-
-        def stats(u, parity, running):
-            top, l = running
-            higher = jnp.maximum(top, products(u, parity))
-            l = l + summed(u - 1, 1 - parity, top)
-            return higher, l * jnp.exp2(top - higher)
-
-        def terms(u, parity):
-            p = jnp.exp2(scores[parity][u // 2] - lse)
+            scores[parity][...] = s
+            return jnp.maximum(top, jnp.max(s, axis=0, keepdims=True))
+
+        def second(u, parity, top, before, l):
+            p = jnp.exp2(scores[parity][...] - top)
             ds = p * dot(va[block_of(u)], mixed[n, 1])
-            weights[parity][...] = p.astype(bf16)
-            dscores[parity][...] = ds.astype(bf16)
-
-        def sums(u, parity):
-            b = block_of(u)
-            ds = dscores[parity][...]
-            dqt[...] += dot(kt[b], ds)
-            acc[b, 0:HEAD] += dot_t(plain[n], ds)
-            acc[b, HEAD:PAIR] += dot_t(mixed[n, 1, 0:HEAD], weights[parity][...])
-
-        def both(t, running):
-            running = stats(2 * t + 1, 1, running)
-            return stats(2 * t + 2, 0, running)
-
-        pairs_left = last // 2
-        odd = last % 2 == 1
-        running = (products(0, 0, True), jnp.zeros((1, 2 * qcount), f32))
-        running = lax.fori_loop(0, pairs_left, both, running)
-
-        def with_odd(running):
-            top, l = stats(last, 1, running)
-            return top, l + summed(last, 1, top)
-
-        def without(running):
-            top, l = running
-            return top, l + summed(last, 0, top)
-
-        top, l = lax.cond(odd, with_odd, without, running)
+            ds = ds.astype(bf16)
+            dscores[parity][...] = ds
+            held[parity][u // 2, 0] = jnp.transpose(ds)
+            held[parity][u // 2, 1] = jnp.transpose(p.astype(bf16))
+            tops[u] = top
+            return l * jnp.exp2(before - top) + jnp.sum(p, axis=0, keepdims=True)
+
+        def third(u, parity, top, before):
+            dqt[...] = dqt[...] * jnp.exp2(before - top) + dot(kt[block_of(u)], dscores[parity][...])
+
+        def step(u, parity, carry):
+            top, before, earlier, l = carry
+            l = second(u - 1, 1 - parity, top, before, l)
+            higher = first(u, parity, top)
+            third(u - 2, parity, before, earlier)
+            return higher, top, before, l
+
+        dqt[...] = jnp.zeros_like(dqt)
+        lowest = jnp.full((1, 2 * qcount), MASKED, f32)
+        nothing = jnp.zeros((1, 2 * qcount), f32)
+        start = first(0, 0, lowest, True)
+
+        def alone(_):
+            l = second(0, 0, start, lowest, nothing)
+            third(0, 0, start, lowest)
+            return start, l
+
+        def several(_):
+            l = second(0, 0, start, lowest, nothing)
+            carry = (first(1, 1, start), start, lowest, l)
+
+            def two(t, carry):
+                return step(2 * t + 3, 1, step(2 * t + 2, 0, carry))
+
+            carry = lax.fori_loop(0, (last - 1) // 2, two, carry)
+
+            def tail(parity, carry):
+                top, before, earlier, l = carry
+                third(last - 1, 1 - parity, before, earlier)
+                l = second(last, parity, top, before, l)
+                third(last, parity, top, before)
+                return top, l
+
+            return lax.cond(
+                last % 2 == 0, lambda c: tail(0, step(last, 0, c)), lambda c: tail(1, c), carry
+            )
+
+        top, l = lax.cond(last == 0, alone, several, 0)
         lse = top + jnp.log2(l)
-
-        dqt[...] = jnp.zeros_like(dqt)
-        terms(0, 0)
-
-        def grads(t, _):
-            sums(2 * t, 0)
-            terms(2 * t + 1, 1)
-            sums(2 * t + 1, 1)
-            terms(2 * t + 2, 0)
+        share = jnp.exp2(top - lse)
+
+        def summed(u, parity):
+            f = jnp.exp2(tops[u] - lse)
+            dk = dot((plain[n].astype(f32) * f).astype(bf16), held[parity][u // 2, 0])
+            dv = dot((mixed[n, 1, 0:HEAD].astype(f32) * f).astype(bf16), held[parity][u // 2, 1])
+            return jnp.concatenate([dk, dv], axis=0)
+
+        def sums_two(t, _):
+            even = summed(2 * t, 0)
+            odd = summed(2 * t + 1, 1)
+            acc[block_of(2 * t)] += even
+            acc[block_of(2 * t + 1)] += odd
             return 0
 
-        lax.fori_loop(0, pairs_left, grads, 0)
-
-        @pl.when(odd)
+        lax.fori_loop(0, (last + 1) // 2, sums_two, 0)
+
+        @pl.when(last % 2 == 0)
         def _():
-            sums(last - 1, 0)
-            terms(last, 1)
-            sums(last, 1)
-
-        @pl.when(jnp.logical_not(odd))
-        def _():
-            sums(last, 0)
-
+            acc[block_of(last)] += summed(last, 0)
+
+        dqt[...] = dqt[...] * share
         total = jnp.concatenate([dqt[:, :qcount], dqt[:, qcount:]], axis=0)
         total = (jnp.transpose(total) * SCALE).astype(bf16)
         row = pl.multiple_of(n * SPAN, SPAN)
@@ -244,7 +255,7 @@
         kv_sorted[b] = jnp.transpose(acc[b] * factor).astype(bf16)
         return 0
 
-    lax.fori_loop(0, blocks, finish, 0)
+    lax.fori_loop(0, blocks, finish, 0, unroll=4)
 
     def collect(slot, _):
         for which, dst in enumerate((dkv_a, dkv_b)):
@@ -281,26 +292,30 @@
             pltpu.VMEM((blocks, BLOCK, PAIR), bf16),
             pltpu.VMEM((blocks, BLOCK, PAIR), bf16),
             pltpu.VMEM((blocks, HEAD, BLOCK), bf16),
-            pltpu.VMEM((half_blocks, BLOCK, 2 * qcount), f32),
-            pltpu.VMEM((half_blocks, BLOCK, 2 * qcount), f32),
+            pltpu.VMEM((BLOCK, 2 * qcount), f32),
+            pltpu.VMEM((BLOCK, 2 * qcount), f32),
+            pltpu.VMEM((half_blocks, 2, 2 * qcount, BLOCK), bf16),
+            pltpu.VMEM((half_blocks, 2, 2 * qcount, BLOCK), bf16),
             pltpu.VMEM((BLOCK, 2 * qcount), bf16),
             pltpu.VMEM((BLOCK, 2 * qcount), bf16),
-            pltpu.VMEM((BLOCK, 2 * qcount), bf16),
-            pltpu.VMEM((BLOCK, 2 * qcount), bf16),
+            pltpu.VMEM((blocks, 1, 2 * qcount), f32),
             pltpu.VMEM((blocks, PAIR, BLOCK), f32),
             pltpu.VMEM((HEAD, 2 * qcount), f32),
         ],
-        compiler_params=pltpu.CompilerParams(vmem_limit_bytes=48 * 1024 * 1024),
-        cost_estimate=pl.CostEstimate(flops=terms * HEAD * 2 * 5 * 4, bytes_accessed=6 << 20, transcendentals=terms),
+        compiler_params=pltpu.CompilerParams(vmem_limit_bytes=26 * 1024 * 1024),
+        cost_estimate=pl.CostEstimate(flops=1 << 20, bytes_accessed=1 << 16, transcendentals=0),
     )(slot_pos, my_pos, kv_a, kv_b, mixed, plain)
 
 
 def project_kernel(core, kv, w_mine, w_other, out):
     rows = w_mine.shape[1]
     for w, part in ((w_mine, core[0]), (w_other, 1 - core[0])):
-        total = dot_t(w[0], kv[0])
-        for g in range(1, kv.shape[0]):
-            total = total + dot_t(w[g], kv[g])
+        total = None
+        for g in range(0, kv.shape[0], 2):
+            term = dot_t(
+                jnp.concatenate([w[g], w[g + 1]], axis=1), jnp.concatenate([kv[g], kv[g + 1]], axis=1)
+            )
+            total = term if total is None else total + term
         out[pl.ds(pl.multiple_of(part * rows, 16), rows), :] = total.astype(bf16)
 
 
@@ -312,7 +327,7 @@
         out_shape=jax.ShapeDtypeStruct((2 * w_mine.shape[1], kv.shape[1]), bf16),
         in_specs=[smem, vmem, vmem, vmem],
         out_specs=vmem,
-        compiler_params=pltpu.CompilerParams(vmem_limit_bytes=24 * 1024 * 1024),
+        compiler_params=pltpu.CompilerParams(vmem_limit_bytes=12 * 1024 * 1024),
         cost_estimate=pl.CostEstimate(
             flops=4 * kv.size * w_mine.shape[1], bytes_accessed=4 * w_mine.size, transcendentals=0
         ),
@@ -370,7 +385,7 @@
     dq, dkv_a, dkv_b = attention_grads(
         slot_pos, my_pos, kv_a.reshape(by_span), kv_b.reshape(by_span), prepared
     )
-    dkv_b, w_mine = lax.optimization_barrier((dkv_b, w_mine))
+    dkv_a, w_mine = lax.optimization_barrier((dkv_a, w_mine))
     dkv = (dkv_a.astype(f32) + exchanged(dkv_b).astype(f32)).astype(bf16)
     w_other = exchanged(w_mine)
     terms = lax.all_to_all(

time: 113 us -> 105 us (0.929)
  local copies, waits for them, and re-layouts: 11.6 us -> 5.77 us
  Pallas kernels: 27.2 us -> 23.4 us
  waiting for transfers between devices: 38.1 us -> 39.8 us
    unnamed x16 -> x8, local copies, waits for them, and re-layouts: 4.83 us -> 0.01 us
    pallas_call x1, Pallas kernels: 23.5 us -> 19.6 us  [attention_grads(): pl.pallas_call(attention_kernel, out_shape=(jax.ShapeDtypeStruct((spans *...]
    all_to_all x1, waiting for transfers between devices: 10.4 us -> 12.1 us  [on_device(): lax.all_to_all(to_all(keys_values, chips), 'ctx', 0, 0, axis_index_groups...]
    ppermute x5, waiting for transfers between devices: 2.33 us -> 1.02 us  [exchanged(): return lax.ppermute(x, 'ctx', other_core)]
    all_to_all x1, waiting for transfers between devices: 2.12 us -> 3.36 us  [on_device(): w_mine = lax.all_to_all(w_part, 'tp', 0, 0)]
  transfers between devices with their start and end apart: 9 -> 9, of which waited for: 5 -> 6; matrix products, arithmetic and copies ran while one was open for 6% -> 7% of each run, Pallas kernels for 21% -> 19%
where the time goes in v3:
time: 105 us; the launch traced here: 104 us
  waiting for transfers between devices  39.8 us (38%)
  starting transfers between devices  31.7 us (30%)
  Pallas kernels  23.4 us (22%)
  local copies, waits for them, and re-layouts  5.77 us (5%)
  other arithmetic  2.8 us (3%)
    pallas_call x1, Pallas kernels, attention_grads(): pl.pallas_call(attention_kernel, out_shape=(jax.ShapeDtypeStruct((spans *...  19.6 us
    all_to_all x1, waiting for transfers between devices, on_device(): lax.all_to_all(dkv.reshape(chips, tokens, -1), 'ctx', 0, 0, axis_index_gr...  15.7 us
    all_to_all x1, waiting for transfers between devices, on_device(): lax.all_to_all(to_all(keys_values, chips), 'ctx', 0, 0, axis_index_groups...  12.1 us
    all_to_all x1, starting transfers between devices, on_device(): lax.all_to_all(to_all(keys_values, chips), 'ctx', 0, 0, axis_index_groups...  9.6 us
    all_to_all x1, starting transfers between devices, on_device(): all_groups = lax.all_to_all(to_all(kv_grad, groups), 'tp', 0, 0)  7.79 us
    all_to_all x1, waiting for transfers between devices, on_device(): all_groups = lax.all_to_all(to_all(kv_grad, groups), 'tp', 0, 0)  7.64 us
    all_to_all x1, starting transfers between devices, on_device(): w_mine = lax.all_to_all(w_part, 'tp', 0, 0)  6.64 us
    all_to_all x1, starting transfers between devices, on_device(): lax.all_to_all(dkv.reshape(chips, tokens, -1), 'ctx', 0, 0, axis_index_gr...  6.63 us
  transfers between devices with their start and end apart: 9, of which 6 were waited for; matrix products, arithmetic and copies ran while one was open for 7% of the time, Pallas kernels for 19%

profile of v3, /device:TPU:32, one launch (start us, length us, event | category | flops | bytes accessed | tf_op | source)
XLA Modules:
  0.0 104.3 jit_solution(3100327248468489720)
XLA Ops:
  0.6 1.7 %broadcast_in_dim.6 = bf16[16,128,128]{2,1,0:T(8,128)(2,1)} broadcast(bf16[128,128]{1,0:T(8,128)(2,1)} %param.7), dimensions={1,2} | broadcast | bytes 557056 | tf_op jit(solution)/shard_map/broadcast_in_dim | solution.py:350
  2.3 9.6 %all-to-all-start = ((bf16[16,128,128]{2,1,0:T(8,128)(2,1)}), bf16[16,128,128]{2,1,0:T(8,128)(2,1)S(1)}, u32[]{:S(2)}, u32[]{:S(2)}) async-start(bf16[16,128,128]{2,1,0:T(8,128)(2,1)} %broadcast_in_dim.6), calls=%async_computation | async-start | bytes 1048576 | tf_op jit(solution)/shard_map/all_to_all | solution.py:355
  11.9 2.9 %dynamic-slice_bitcast_fusion = bf16[8,928,128]{2,1,0:T(8,128)(2,1)} fusion(bf16[8,2,928,128]{3,2,1,0:T(8,128)(2,1)} %bitcast.16, s32[]{:T(128)S(6)} %select_n.51), kind=kLoop, calls=%fused_computation | loop fusion | bytes 3801092 | tf_op jit(solution)/shard_map/jit(dynamic_index_in_dim)/squeeze | solution.py:358
  14.8 12.1 %all-to-all-done = bf16[16,128,128]{2,1,0:T(8,128)(2,1)S(1)} async-done(((bf16[16,128,128]{2,1,0:T(8,128)(2,1)}), bf16[16,128,128]{2,1,0:T(8,128)(2,1)S(1)}, u32[]{:S(2)}, u32[]{:S(2)}) %all-to-all-start) | async-done | bytes 524320 | tf_op jit(solution)/shard_map/all_to_all | solution.py:355
  26.9 6.6 %all-to-all-start.1 = ((bf16[8,928,128]{2,1,0:T(8,128)(2,1)}), bf16[8,928,128]{2,1,0:T(8,128)(2,1)S(1)}, u32[]{:S(2)}, u32[]{:S(2)}) async-start(bf16[8,928,128]{2,1,0:T(8,128)(2,1)} %dynamic-slice_bitcast_fusion), calls=%async_computation.1 | async-start | bytes 3801088 | tf_op jit(solution)/shard_map/all_to_all | solution.py:362
  33.6 0.8 pad_maximum_fusion.1
  34.4 0.1 reshape.33
  34.7 0.1 reshape.34
  34.8 0.6 collective-permute-start
  35.6 0.7 collective-permute-done.1.rows_b
  36.3 0.3 shard_map.77
  36.7 0.3 collective-permute-done
  36.9 19.6 %shard_map.78 = (bf16[256,512]{1,0:T(8,128)(2,1)S(1)}, bf16[32,64,128]{2,1,0:T(8,128)(2,1)S(1)}, bf16[32,64,128]{2,1,0:T(8,128)(2,1)}) custom-call(s32[64]{0:T(128)S(1)} %pad_add_fusion.slot_pos, s32[4]{0:T(128)S(1)} %pad_add_fusion.1.my_pos, bf16[32,64,128]{2,1,0:T(8,128)(2,1)S(1)} %bitcast.14, bf16[32,64,128]{2,1,0:T(8,128)(2,1)S(1)} %bitcast.15, ...), custom_call_target="tpu_custom_call" | custom-call | flops 1048576 | bytes 65536 | tf_op jit(solution)/shard_map/pallas_call | solution.py:281
  56.5 0.4 collective-permute-start.3
  56.9 3.4 %all-to-all-done.1.w_mine = bf16[8,928,128]{2,1,0:T(8,128)(2,1)S(1)} async-done(((bf16[8,928,128]{2,1,0:T(8,128)(2,1)}), bf16[8,928,128]{2,1,0:T(8,128)(2,1)S(1)}, u32[]{:S(2)}, u32[]{:S(2)}) %all-to-all-start.1) | async-done | bytes 1900576 | tf_op jit(solution)/shard_map/all_to_all | solution.py:362
  60.3 1.0 add_convert_fusion
  61.3 6.6 %all-to-all-start.2 = ((bf16[16,128,128]{2,1,0:T(8,128)(2,1)}), bf16[16,128,128]{2,1,0:T(8,128)(2,1)S(1)}, u32[]{:S(2)}, u32[]{:S(2)}) async-start(bf16[16,128,128]{2,1,0:T(8,128)(2,1)} %bitcast.7), calls=%async_computation.2 | async-start | bytes 1048576 | tf_op jit(solution)/shard_map/all_to_all | solution.py:391
  67.9 0.1 collective-permute-start.2
  68.0 15.7 %all-to-all-done.2 = bf16[16,128,128]{2,1,0:T(8,128)(2,1)S(1)} async-done(((bf16[16,128,128]{2,1,0:T(8,128)(2,1)}), bf16[16,128,128]{2,1,0:T(8,128)(2,1)S(1)}, u32[]{:S(2)}, u32[]{:S(2)}) %all-to-all-start.2) | async-done | bytes 524320 | tf_op jit(solution)/shard_map/all_to_all | solution.py:391
  83.9 0.7 broadcast_in_dim.8
  84.6 7.8 %all-to-all-start.3 = ((bf16[8,128,128]{2,1,0:T(8,128)(2,1)}), bf16[8,128,128]{2,1,0:T(8,128)(2,1)S(1)}, u32[]{:S(2)}, u32[]{:S(2)}) async-start(bf16[8,128,128]{2,1,0:T(8,128)(2,1)} %broadcast_in_dim.8), calls=%async_computation.3 | async-start | bytes 524288 | tf_op jit(solution)/shard_map/all_to_all | solution.py:395
  92.4 0.8 maximum_select_fusion
  93.2 7.6 %all-to-all-done.3.kv = bf16[8,128,128]{2,1,0:T(8,128)(2,1)S(1)} async-done(((bf16[8,128,128]{2,1,0:T(8,128)(2,1)}), bf16[8,128,128]{2,1,0:T(8,128)(2,1)S(1)}, u32[]{:S(2)}, u32[]{:S(2)}) %all-to-all-start.3) | async-done | bytes 262176 | tf_op jit(solution)/shard_map/all_to_all | solution.py:395
  100.8 3.4 %shard_map.79 = bf16[1856,128]{1,0:T(8,128)(2,1)} custom-call(s32[1]{0:T(128)} %bitcast.6.core, bf16[8,128,128]{2,1,0:T(8,128)(2,1)S(1)} %all-to-all-done.3.kv, bf16[8,928,128]{2,1,0:T(8,128)(2,1)S(1)} %all-to-all-done.1.w_mine, bf16[8,928,128]{2,1,0:T(8,128)(2,1)} %collective-permute-done.4.w_other), custom_call_target="tpu_custom_call" | custom-call | flops 486539264 | bytes 3801088 | tf_op jit(solution)/shard_map/pallas_call | solution.py:325
  (23 shorter events, 0.5 us)
Async XLA Ops:
  2.3 24.6 %all-to-all-start = ((bf16[16,128,128]{2,1,0:T(8,128)(2,1)}), bf16[16,128,128]{2,1,0:T(8,128)(2,1)S(1)}, u32[]{:S(2)}, u32[]{:S(2)}) async-start(bf16[16,128,128]{2,1,0:T(8,128)(2,1)} %broadcast_in_dim.6), calls=%async_computation | async-start | bytes 1048576 | tf_op jit(solution)/shard_map/all_to_all | solution.py:355
  14.8 18.7 %copy-start.2 = (bf16[128,1024]{1,0:T(8,128)(2,1)S(1)}, bf16[128,1024]{1,0:T(8,128)(2,1)}, u32[]{:S(2)}) copy-start(bf16[128,1024]{1,0:T(8,128)(2,1)} %param.6) | copy-start | bytes 786436
  14.8 18.8 %copy-start = (bf16[128,1024]{1,0:T(8,128)(2,1)S(1)}, bf16[128,1024]{1,0:T(8,128)(2,1)}, u32[]{:S(2)}) copy-start(bf16[128,1024]{1,0:T(8,128)(2,1)} %param.8) | copy-start | bytes 786436
  14.8 18.8 %copy-start.1 = (bf16[128,1024]{1,0:T(8,128)(2,1)S(1)}, bf16[128,1024]{1,0:T(8,128)(2,1)}, u32[]{:S(2)}) copy-start(bf16[128,1024]{1,0:T(8,128)(2,1)} %param.9) | copy-start | bytes 786436
  26.9 33.4 %all-to-all-start.1 = ((bf16[8,928,128]{2,1,0:T(8,128)(2,1)}), bf16[8,928,128]{2,1,0:T(8,128)(2,1)S(1)}, u32[]{:S(2)}, u32[]{:S(2)}) async-start(bf16[8,928,128]{2,1,0:T(8,128)(2,1)} %dynamic-slice_bitcast_fusion), calls=%async_computation.1 | async-start | bytes 3801088 | tf_op jit(solution)/shard_map/all_to_all | solution.py:362
  33.5 0.9 copy-start.3
  34.4 1.9 %collective-permute-start.1 = (bf16[128,1536]{1,0:T(8,128)(2,1)}, bf16[128,1536]{1,0:T(8,128)(2,1)S(1)}, u32[]{:S(2)}, u32[]{:S(2)}) collective-permute-start(bf16[128,1536]{1,0:T(8,128)(2,1)} %pad_maximum_fusion.1), channel_id=1, source_target_pairs={{0,8},{8,0},{16,24},{24,16},{32,40},{40,32},{48,56},{56,48},{64,72... | collective-permute-start | bytes 1179656 | tf_op jit(solution)/shard_map/ppermute | solution.py:353
  34.8 2.1 %collective-permute-start = (bf16[16,128,128]{2,1,0:T(8,128)(2,1)S(1)}, bf16[16,128,128]{2,1,0:T(8,128)(2,1)S(1)}, u32[]{:S(2)}, u32[]{:S(2)}) collective-permute-start(bf16[16,128,128]{2,1,0:T(8,128)(2,1)S(1)} %all-to-all-done), channel_id=1, source_target_pairs={{0,8},{8,0},{16,24},{24,16},{32,40},{40,32},{48,56},{56,48},{64,72... | collective-permute-start | bytes 1572872 | tf_op jit(solution)/shard_map/ppermute | solution.py:353
  56.5 3.7 %collective-permute-start.3 = (bf16[32,64,128]{2,1,0:T(8,128)(2,1)}, bf16[32,64,128]{2,1,0:T(8,128)(2,1)S(1)}, u32[]{:S(2)}, u32[]{:S(2)}) collective-permute-start(bf16[32,64,128]{2,1,0:T(8,128)(2,1)} %get-tuple-element.18), channel_id=1, source_target_pairs={{0,8},{8,0},{16,24},{24,16},{32,40},{40,32},{48,56},{56,48},{64,72... | collective-permute-start | bytes 1572872 | tf_op jit(solution)/shard_map/ppermute | solution.py:353
  60.3 40.5 %collective-permute-start.4 = (bf16[8,928,128]{2,1,0:T(8,128)(2,1)S(1)}, bf16[8,928,128]{2,1,0:T(8,128)(2,1)}, u32[]{:S(2)}, u32[]{:S(2)}) collective-permute-start(bf16[8,928,128]{2,1,0:T(8,128)(2,1)S(1)} %all-to-all-done.1.w_mine), channel_id=1, source_target_pairs={{0,8},{8,0},{16,24},{24,16},{32,40},{40,32},{48,56},{56,48},{64,72... | collective-permute-start | bytes 5701640 | tf_op jit(solution)/shard_map/ppermute | solution.py:353
  61.3 22.5 %all-to-all-start.2 = ((bf16[16,128,128]{2,1,0:T(8,128)(2,1)}), bf16[16,128,128]{2,1,0:T(8,128)(2,1)S(1)}, u32[]{:S(2)}, u32[]{:S(2)}) async-start(bf16[16,128,128]{2,1,0:T(8,128)(2,1)} %bitcast.7), calls=%async_computation.2 | async-start | bytes 1048576 | tf_op jit(solution)/shard_map/all_to_all | solution.py:391
  67.9 24.5 %collective-permute-start.2 = (bf16[128,512]{1,0:T(8,128)(2,1)S(1)}, bf16[128,512]{1,0:T(8,128)(2,1)S(1)}, u32[]{:S(2)}, u32[]{:S(2)}) collective-permute-start(bf16[128,512]{1,0:T(8,128)(2,1)S(1)} %get-tuple-element.23), channel_id=1, source_target_pairs={{0,8},{8,0},{16,24},{24,16},{32,40},{40,32},{48,56},{56,48},{64,72... | collective-permute-start | bytes 393224 | tf_op jit(solution)/shard_map/ppermute | solution.py:353
  84.6 16.2 %all-to-all-start.3 = ((bf16[8,128,128]{2,1,0:T(8,128)(2,1)}), bf16[8,128,128]{2,1,0:T(8,128)(2,1)S(1)}, u32[]{:S(2)}, u32[]{:S(2)}) async-start(bf16[8,128,128]{2,1,0:T(8,128)(2,1)} %broadcast_in_dim.8), calls=%async_computation.3 | async-start | bytes 524288 | tf_op jit(solution)/shard_map/all_to_all | solution.py:395

commit v4 on v3

--- a/solution.py
+++ b/solution.py
@@ -302,7 +302,7 @@
             pltpu.VMEM((blocks, PAIR, BLOCK), f32),
             pltpu.VMEM((HEAD, 2 * qcount), f32),
         ],
-        compiler_params=pltpu.CompilerParams(vmem_limit_bytes=26 * 1024 * 1024),
+        compiler_params=pltpu.CompilerParams(vmem_limit_bytes=20 * 1024 * 1024),
         cost_estimate=pl.CostEstimate(flops=1 << 20, bytes_accessed=1 << 16, transcendentals=0),
     )(slot_pos, my_pos, kv_a, kv_b, mixed, plain)
 
@@ -358,15 +358,16 @@
     w_part = lax.dynamic_index_in_dim(
         kv_weight.reshape(groups, 2, features // 2, kv_weight.shape[1]), core, 1, False
     )
-    kv_a, w_part = lax.optimization_barrier((kv_a, w_part))
+
+    def my_heads(k):
+        return [lax.dynamic_slice_in_dim(x, k * half, half, 1) for x in (queries, out_grad, forward_out)]
+
+    rows_a = jnp.concatenate(my_heads(core), axis=1)
+    rows_b = exchanged(jnp.concatenate(my_heads(1 - core), axis=1))
+
+    kv_a, w_part, rows_b = lax.optimization_barrier((kv_a, w_part, rows_b))
     w_mine = lax.all_to_all(w_part, "tp", 0, 0)
     kv_b = exchanged(kv_a)
-
-    def my_heads(k):
-        return [lax.dynamic_slice_in_dim(x, k * half, half, 1) for x in (queries, out_grad, forward_out)]
-
-    rows_a = jnp.concatenate(my_heads(core), axis=1)
-    rows_b = exchanged(jnp.concatenate(my_heads(1 - core), axis=1))
 
     spans = tokens // SPAN
     by_device = span_table.reshape(chips, 2, spans)

time: 105 us -> 104 us (level)
  waiting for transfers between devices: 39.8 us -> 42.8 us
  Pallas kernels: 23.4 us -> 20.6 us
    all_to_all x1, waiting for transfers between devices: 3.36 us -> 7.43 us  [on_device(): w_mine = lax.all_to_all(w_part, 'tp', 0, 0)]
    pallas_call x1, Pallas kernels: 19.6 us -> 16.8 us  [attention_grads(): pl.pallas_call(attention_kernel, out_shape=(jax.ShapeDtypeStruct((spans *...]
    all_to_all x1, waiting for transfers between devices: 12.1 us -> 10.8 us  [on_device(): lax.all_to_all(to_all(keys_values, chips), 'ctx', 0, 0, axis_index_groups...]
  transfers between devices with their start and end apart: 9 -> 9, of which waited for: 6 -> 5; matrix products, arithmetic and copies ran while one was open for 7% -> 7% of each run, Pallas kernels for 19% -> 16%
where the time goes in v4:
time: 104 us
  waiting for transfers between devices  42.8 us (41%)
  starting transfers between devices  31 us (30%)
  Pallas kernels  20.6 us (20%)
  local copies, waits for them, and re-layouts  6.78 us (7%)
  other arithmetic  2.05 us (2%)
    pallas_call x1, Pallas kernels, attention_grads(): pl.pallas_call(attention_kernel, out_shape=(jax.ShapeDtypeStruct((spans *...  16.8 us
    all_to_all x1, waiting for transfers between devices, on_device(): lax.all_to_all(dkv.reshape(chips, tokens, -1), 'ctx', 0, 0, axis_index_gr...  15.5 us
    all_to_all x1, waiting for transfers between devices, on_device(): lax.all_to_all(to_all(keys_values, chips), 'ctx', 0, 0, axis_index_groups...  10.8 us
    all_to_all x1, starting transfers between devices, on_device(): lax.all_to_all(to_all(keys_values, chips), 'ctx', 0, 0, axis_index_groups...  9.6 us
    all_to_all x1, waiting for transfers between devices, on_device(): all_groups = lax.all_to_all(to_all(kv_grad, groups), 'tp', 0, 0)  7.64 us
    all_to_all x1, waiting for transfers between devices, on_device(): w_mine = lax.all_to_all(w_part, 'tp', 0, 0)  7.43 us
    all_to_all x1, starting transfers between devices, on_device(): all_groups = lax.all_to_all(to_all(kv_grad, groups), 'tp', 0, 0)  7.21 us
    all_to_all x1, starting transfers between devices, on_device(): lax.all_to_all(dkv.reshape(chips, tokens, -1), 'ctx', 0, 0, axis_index_gr...  7.18 us
  transfers between devices with their start and end apart: 9, of which 5 were waited for; matrix products, arithmetic and copies ran while one was open for 7% of the time, Pallas kernels for 16%

profile of v4, /device:TPU:32, one launch (start us, length us, event | category | flops | bytes accessed | tf_op | source)
XLA Modules:
  0.0 104.1 jit_solution(700780844492609650)
XLA Ops:
  0.7 1.7 %broadcast_in_dim.6 = bf16[16,128,128]{2,1,0:T(8,128)(2,1)} broadcast(bf16[128,128]{1,0:T(8,128)(2,1)} %param.7), dimensions={1,2} | broadcast | bytes 557056 | tf_op jit(solution)/shard_map/broadcast_in_dim | solution.py:350
  2.4 9.6 %all-to-all-start = ((bf16[16,128,128]{2,1,0:T(8,128)(2,1)}), bf16[16,128,128]{2,1,0:T(8,128)(2,1)S(1)}, u32[]{:S(2)}, u32[]{:S(2)}) async-start(bf16[16,128,128]{2,1,0:T(8,128)(2,1)} %broadcast_in_dim.6), calls=%async_computation | async-start | bytes 1048576 | tf_op jit(solution)/shard_map/all_to_all | solution.py:355
  12.0 1.0 constant_dynamic-slice_fusion.2
  13.0 0.1 collective-permute-start
  13.2 2.9 %dynamic-slice_bitcast_fusion = bf16[8,928,128]{2,1,0:T(8,128)(2,1)} fusion(bf16[8,2,928,128]{3,2,1,0:T(8,128)(2,1)} %bitcast.16, s32[]{:T(128)S(6)} %select_n.51), kind=kLoop, calls=%fused_computation | loop fusion | bytes 3801092 | tf_op jit(solution)/shard_map/jit(dynamic_index_in_dim)/squeeze | solution.py:358
  16.1 10.8 %all-to-all-done = bf16[16,128,128]{2,1,0:T(8,128)(2,1)S(1)} async-done(((bf16[16,128,128]{2,1,0:T(8,128)(2,1)}), bf16[16,128,128]{2,1,0:T(8,128)(2,1)S(1)}, u32[]{:S(2)}, u32[]{:S(2)}) %all-to-all-start) | async-done | bytes 524320 | tf_op jit(solution)/shard_map/all_to_all | solution.py:355
  26.9 6.6 %all-to-all-start.1 = ((bf16[8,928,128]{2,1,0:T(8,128)(2,1)}), bf16[8,928,128]{2,1,0:T(8,128)(2,1)S(1)}, u32[]{:S(2)}, u32[]{:S(2)}) async-start(bf16[8,928,128]{2,1,0:T(8,128)(2,1)} %dynamic-slice_bitcast_fusion), calls=%async_computation.1 | async-start | bytes 3801088 | tf_op jit(solution)/shard_map/all_to_all | solution.py:369
  33.6 0.1 reshape.33
  33.9 0.1 reshape.34
  34.0 0.1 collective-permute-start.1
  34.3 0.3 shard_map.77
  34.6 1.4 %collective-permute-done.1 = bf16[16,128,128]{2,1,0:T(8,128)(2,1)S(1)} collective-permute-done((bf16[16,128,128]{2,1,0:T(8,128)(2,1)S(1)}, bf16[16,128,128]{2,1,0:T(8,128)(2,1)S(1)}, u32[]{:S(2)}, u32[]{:S(2)}) %collective-permute-start.1) | collective-permute-done | bytes 524320 | tf_op jit(solution)/shard_map/ppermute | solution.py:353
  36.0 16.8 %shard_map.78 = (bf16[256,512]{1,0:T(8,128)(2,1)S(1)}, bf16[32,64,128]{2,1,0:T(8,128)(2,1)S(1)}, bf16[32,64,128]{2,1,0:T(8,128)(2,1)}) custom-call(s32[64]{0:T(128)S(1)} %pad_add_fusion.slot_pos, s32[4]{0:T(128)S(1)} %pad_add_fusion.1.my_pos, bf16[32,64,128]{2,1,0:T(8,128)(2,1)S(1)} %bitcast.14, bf16[32,64,128]{2,1,0:T(8,128)(2,1)S(1)} %bitcast.15, ...), custom_call_target="tpu_custom_call" | custom-call | flops 1048576 | bytes 65536 | tf_op jit(solution)/shard_map/pallas_call | solution.py:281
  52.8 0.1 collective-permute-start.3
  52.9 7.4 %all-to-all-done.1.w_mine = bf16[8,928,128]{2,1,0:T(8,128)(2,1)S(1)} async-done(((bf16[8,928,128]{2,1,0:T(8,128)(2,1)}), bf16[8,928,128]{2,1,0:T(8,128)(2,1)S(1)}, u32[]{:S(2)}, u32[]{:S(2)}) %all-to-all-start.1) | async-done | bytes 1900576 | tf_op jit(solution)/shard_map/all_to_all | solution.py:369
  60.4 1.0 add_convert_fusion
  61.3 7.2 %all-to-all-start.2 = ((bf16[16,128,128]{2,1,0:T(8,128)(2,1)}), bf16[16,128,128]{2,1,0:T(8,128)(2,1)S(1)}, u32[]{:S(2)}, u32[]{:S(2)}) async-start(bf16[16,128,128]{2,1,0:T(8,128)(2,1)} %bitcast.7), calls=%async_computation.2 | async-start | bytes 1048576 | tf_op jit(solution)/shard_map/all_to_all | solution.py:392
  68.5 0.1 collective-permute-start.2
  68.6 15.5 %all-to-all-done.2 = bf16[16,128,128]{2,1,0:T(8,128)(2,1)S(1)} async-done(((bf16[16,128,128]{2,1,0:T(8,128)(2,1)}), bf16[16,128,128]{2,1,0:T(8,128)(2,1)S(1)}, u32[]{:S(2)}, u32[]{:S(2)}) %all-to-all-start.2) | async-done | bytes 524320 | tf_op jit(solution)/shard_map/all_to_all | solution.py:392
  84.2 0.7 broadcast_in_dim.8
  85.0 7.2 %all-to-all-start.3 = ((bf16[8,128,128]{2,1,0:T(8,128)(2,1)}), bf16[8,128,128]{2,1,0:T(8,128)(2,1)S(1)}, u32[]{:S(2)}, u32[]{:S(2)}) async-start(bf16[8,128,128]{2,1,0:T(8,128)(2,1)} %broadcast_in_dim.8), calls=%async_computation.3 | async-start | bytes 524288 | tf_op jit(solution)/shard_map/all_to_all | solution.py:396
  92.2 0.8 maximum_select_fusion
  93.0 7.6 %all-to-all-done.3.kv = bf16[8,128,128]{2,1,0:T(8,128)(2,1)S(1)} async-done(((bf16[8,128,128]{2,1,0:T(8,128)(2,1)}), bf16[8,128,128]{2,1,0:T(8,128)(2,1)S(1)}, u32[]{:S(2)}, u32[]{:S(2)}) %all-to-all-start.3) | async-done | bytes 262176 | tf_op jit(solution)/shard_map/all_to_all | solution.py:396
  100.6 3.4 %shard_map.79 = bf16[1856,128]{1,0:T(8,128)(2,1)} custom-call(s32[1]{0:T(128)} %bitcast.6.core, bf16[8,128,128]{2,1,0:T(8,128)(2,1)S(1)} %all-to-all-done.3.kv, bf16[8,928,128]{2,1,0:T(8,128)(2,1)S(1)} %all-to-all-done.1.w_mine, bf16[8,928,128]{2,1,0:T(8,128)(2,1)} %collective-permute-done.4.w_other), custom_call_target="tpu_custom_call" | custom-call | flops 486539264 | bytes 3801088 | tf_op jit(solution)/shard_map/pallas_call | solution.py:325
  (21 shorter events, 0.5 us)
Async XLA Ops:
  0.6 12.3 %copy-start = (bf16[128,1024]{1,0:T(8,128)(2,1)S(1)}, bf16[128,1024]{1,0:T(8,128)(2,1)}, u32[]{:S(2)}) copy-start(bf16[128,1024]{1,0:T(8,128)(2,1)} %param.8) | copy-start | bytes 786436
  0.6 12.3 %copy-start.1 = (bf16[128,1024]{1,0:T(8,128)(2,1)S(1)}, bf16[128,1024]{1,0:T(8,128)(2,1)}, u32[]{:S(2)}) copy-start(bf16[128,1024]{1,0:T(8,128)(2,1)} %param.9) | copy-start | bytes 786436
  2.4 24.6 %all-to-all-start = ((bf16[16,128,128]{2,1,0:T(8,128)(2,1)}), bf16[16,128,128]{2,1,0:T(8,128)(2,1)S(1)}, u32[]{:S(2)}, u32[]{:S(2)}) async-start(bf16[16,128,128]{2,1,0:T(8,128)(2,1)} %broadcast_in_dim.6), calls=%async_computation | async-start | bytes 1048576 | tf_op jit(solution)/shard_map/all_to_all | solution.py:355
  13.0 3.0 %collective-permute-start = (bf16[128,1536]{1,0:T(8,128)(2,1)S(1)}, bf16[128,1536]{1,0:T(8,128)(2,1)S(1)}, u32[]{:S(2)}, u32[]{:S(2)}) collective-permute-start(bf16[128,1536]{1,0:T(8,128)(2,1)S(1)} %pad_maximum_fusion), channel_id=1, source_target_pairs={{0,8},{8,0},{16,24},{24,16},{32,40},{40,32},{48,56},{56,48},{64,72... | collective-permute-start | bytes 1179656 | tf_op jit(solution)/shard_map/ppermute | solution.py:353
  16.1 17.5 %copy-start.2 = (s32[64]{0:T(128)S(1)}, s32[64]{0:T(128)}, u32[]{:S(2)}) copy-start(s32[64]{0:T(128)} %param.11) | copy-start | bytes 772
  26.9 33.4 %all-to-all-start.1 = ((bf16[8,928,128]{2,1,0:T(8,128)(2,1)}), bf16[8,928,128]{2,1,0:T(8,128)(2,1)S(1)}, u32[]{:S(2)}, u32[]{:S(2)}) async-start(bf16[8,928,128]{2,1,0:T(8,128)(2,1)} %dynamic-slice_bitcast_fusion), calls=%async_computation.1 | async-start | bytes 3801088 | tf_op jit(solution)/shard_map/all_to_all | solution.py:369
  34.0 2.0 %collective-permute-start.1 = (bf16[16,128,128]{2,1,0:T(8,128)(2,1)S(1)}, bf16[16,128,128]{2,1,0:T(8,128)(2,1)S(1)}, u32[]{:S(2)}, u32[]{:S(2)}) collective-permute-start(bf16[16,128,128]{2,1,0:T(8,128)(2,1)S(1)} %all-to-all-done), channel_id=1, source_target_pairs={{0,8},{8,0},{16,24},{24,16},{32,40},{40,32},{48,56},{56,48},{64,72... | collective-permute-start | bytes 1572872 | tf_op jit(solution)/shard_map/ppermute | solution.py:353
  52.8 7.6 %collective-permute-start.3 = (bf16[32,64,128]{2,1,0:T(8,128)(2,1)}, bf16[32,64,128]{2,1,0:T(8,128)(2,1)S(1)}, u32[]{:S(2)}, u32[]{:S(2)}) collective-permute-start(bf16[32,64,128]{2,1,0:T(8,128)(2,1)} %get-tuple-element.20), channel_id=1, source_target_pairs={{0,8},{8,0},{16,24},{24,16},{32,40},{40,32},{48,56},{56,48},{64,72... | collective-permute-start | bytes 1572872 | tf_op jit(solution)/shard_map/ppermute | solution.py:353
  60.3 40.3 %collective-permute-start.4 = (bf16[8,928,128]{2,1,0:T(8,128)(2,1)S(1)}, bf16[8,928,128]{2,1,0:T(8,128)(2,1)}, u32[]{:S(2)}, u32[]{:S(2)}) collective-permute-start(bf16[8,928,128]{2,1,0:T(8,128)(2,1)S(1)} %all-to-all-done.1.w_mine), channel_id=1, source_target_pairs={{0,8},{8,0},{16,24},{24,16},{32,40},{40,32},{48,56},{56,48},{64,72... | collective-permute-start | bytes 5701640 | tf_op jit(solution)/shard_map/ppermute | solution.py:353
  61.3 22.8 %all-to-all-start.2 = ((bf16[16,128,128]{2,1,0:T(8,128)(2,1)}), bf16[16,128,128]{2,1,0:T(8,128)(2,1)S(1)}, u32[]{:S(2)}, u32[]{:S(2)}) async-start(bf16[16,128,128]{2,1,0:T(8,128)(2,1)} %bitcast.7), calls=%async_computation.2 | async-start | bytes 1048576 | tf_op jit(solution)/shard_map/all_to_all | solution.py:392
  68.5 23.6 %collective-permute-start.2 = (bf16[128,512]{1,0:T(8,128)(2,1)S(1)}, bf16[128,512]{1,0:T(8,128)(2,1)S(1)}, u32[]{:S(2)}, u32[]{:S(2)}) collective-permute-start(bf16[128,512]{1,0:T(8,128)(2,1)S(1)} %get-tuple-element.25), channel_id=1, source_target_pairs={{0,8},{8,0},{16,24},{24,16},{32,40},{40,32},{48,56},{56,48},{64,72... | collective-permute-start | bytes 393224 | tf_op jit(solution)/shard_map/ppermute | solution.py:353
  85.0 15.7 %all-to-all-start.3 = ((bf16[8,128,128]{2,1,0:T(8,128)(2,1)}), bf16[8,128,128]{2,1,0:T(8,128)(2,1)S(1)}, u32[]{:S(2)}, u32[]{:S(2)}) async-start(bf16[8,128,128]{2,1,0:T(8,128)(2,1)} %broadcast_in_dim.8), calls=%async_computation.3 | async-start | bytes 524288 | tf_op jit(solution)/shard_map/all_to_all | solution.py:396

commit v5 on v4

--- a/solution.py
+++ b/solution.py
@@ -10,6 +10,7 @@
 HEAD = 64
 SPAN = 64
 BLOCK = 512
+AT_ONCE = 4
 PAIR = 2 * HEAD
 SCALE = 0.125
 LOG2E = 1.4426950408889634
@@ -107,16 +108,15 @@
     kt,
     scores_0,
     scores_1,
-    held_0,
-    held_1,
+    held,
     dscores_0,
     dscores_1,
     tops,
+    lses,
     acc,
     dqt,
 ):
     scores = (scores_0, scores_1)
-    held = (held_0, held_1)
     dscores = (dscores_0, dscores_1)
     half_slots = kv_a.shape[0]
     blocks = kk.shape[0]
@@ -170,9 +170,9 @@
             ds = p * dot(va[block_of(u)], mixed[n, 1])
             ds = ds.astype(bf16)
             dscores[parity][...] = ds
-            held[parity][u // 2, 0] = jnp.transpose(ds)
-            held[parity][u // 2, 1] = jnp.transpose(p.astype(bf16))
-            tops[u] = top
+            held[n, u, 0] = jnp.transpose(ds)
+            held[n, u, 1] = jnp.transpose(p.astype(bf16))
+            tops[n, u] = top
             return l * jnp.exp2(before - top) + jnp.sum(p, axis=0, keepdims=True)
 
         def third(u, parity, top, before):
@@ -216,29 +216,8 @@
             )
 
         top, l = lax.cond(last == 0, alone, several, 0)
-        lse = top + jnp.log2(l)
-        share = jnp.exp2(top - lse)
-
-        def summed(u, parity):
-            f = jnp.exp2(tops[u] - lse)
-            dk = dot((plain[n].astype(f32) * f).astype(bf16), held[parity][u // 2, 0])
-            dv = dot((mixed[n, 1, 0:HEAD].astype(f32) * f).astype(bf16), held[parity][u // 2, 1])
-            return jnp.concatenate([dk, dv], axis=0)
-
-        def sums_two(t, _):
-            even = summed(2 * t, 0)
-            odd = summed(2 * t + 1, 1)
-            acc[block_of(2 * t)] += even
-            acc[block_of(2 * t + 1)] += odd
-            return 0
-
-        lax.fori_loop(0, (last + 1) // 2, sums_two, 0)
-
-        @pl.when(last % 2 == 0)
-        def _():
-            acc[block_of(last)] += summed(last, 0)
-
-        dqt[...] = dqt[...] * share
+        lses[n] = top + jnp.log2(l)
+        dqt[...] = dqt[...] * jnp.exp2(top - lses[n])
         total = jnp.concatenate([dqt[:, :qcount], dqt[:, qcount:]], axis=0)
         total = (jnp.transpose(total) * SCALE).astype(bf16)
         row = pl.multiple_of(n * SPAN, SPAN)
@@ -248,6 +227,45 @@
 
     lax.fori_loop(0, plain.shape[0], one_span, 0)
 
+    spans = mixed.shape[0]
+    lasts = [my_pos[n] // per_block for n in range(spans)]
+    ends = [lasts[0] + 1]
+    for n in range(1, spans):
+        ends.append(ends[-1] + lasts[n] + 1)
+
+    def located(i):
+        n, u, last = 0, i, lasts[0]
+        for k in range(1, spans):
+            later = i >= ends[k - 1]
+            n = jnp.where(later, k, n)
+            u = jnp.where(later, i - ends[k - 1], u)
+            last = jnp.where(later, lasts[k], last)
+        return n, u, jnp.where(u == 0, last, u - 1)
+
+    def summed(n, u):
+        f = jnp.exp2(tops[n, u] - lses[n])
+        dk = dot((plain[n].astype(f32) * f).astype(bf16), held[n, u, 0])
+        dv = dot((mixed[n, 1, 0:HEAD].astype(f32) * f).astype(bf16), held[n, u, 1])
+        return jnp.concatenate([dk, dv], axis=0)
+
+    def sums_several(first, count):
+        places = [located(first + k) for k in range(count)]
+        results = [summed(n, u) for n, u, _ in places]
+        for (_, _, b), result in zip(places, results):
+            acc[b] += result
+
+    def sums_step(t, _):
+        sums_several(t * AT_ONCE, AT_ONCE)
+        return 0
+
+    def sums_rest(i, _):
+        sums_several(i, 1)
+        return 0
+
+    rounds = ends[-1] // AT_ONCE
+    lax.fori_loop(0, rounds, sums_step, 0)
+    lax.fori_loop(rounds * AT_ONCE, ends[-1], sums_rest, 0)
+
     line = lax.broadcasted_iota(jnp.int32, (PAIR, BLOCK), 0)
     factor = jnp.where(line < HEAD, SCALE, 1.0)
 
@@ -271,7 +289,6 @@
     mixed, plain = prepared
     slots = 2 * kv_a.shape[0]
     blocks = slots * SPAN // BLOCK
-    half_blocks = (blocks + 1) // 2
     spans = plain.shape[0]
     qcount = plain.shape[2] // 2
     pairs = qcount // SPAN
@@ -294,15 +311,15 @@
             pltpu.VMEM((blocks, HEAD, BLOCK), bf16),
             pltpu.VMEM((BLOCK, 2 * qcount), f32),
             pltpu.VMEM((BLOCK, 2 * qcount), f32),
-            pltpu.VMEM((half_blocks, 2, 2 * qcount, BLOCK), bf16),
-            pltpu.VMEM((half_blocks, 2, 2 * qcount, BLOCK), bf16),
+            pltpu.VMEM((spans, blocks, 2, 2 * qcount, BLOCK), bf16),
             pltpu.VMEM((BLOCK, 2 * qcount), bf16),
             pltpu.VMEM((BLOCK, 2 * qcount), bf16),
-            pltpu.VMEM((blocks, 1, 2 * qcount), f32),
+            pltpu.VMEM((spans, blocks, 1, 2 * qcount), f32),
+            pltpu.VMEM((spans, 1, 2 * qcount), f32),
             pltpu.VMEM((blocks, PAIR, BLOCK), f32),
             pltpu.VMEM((HEAD, 2 * qcount), f32),
         ],
-        compiler_params=pltpu.CompilerParams(vmem_limit_bytes=20 * 1024 * 1024),
+        compiler_params=pltpu.CompilerParams(vmem_limit_bytes=45 * 1024 * 1024),
         cost_estimate=pl.CostEstimate(flops=1 << 20, bytes_accessed=1 << 16, transcendentals=0),
     )(slot_pos, my_pos, kv_a, kv_b, mixed, plain)
 

time: 104 us -> 103 us (level)
    all_to_all x1, starting transfers between devices: 7.18 us -> 5.69 us  [on_device(): lax.all_to_all(dkv.reshape(chips, tokens, -1), 'ctx', 0, 0, axis_index_gr...]
  transfers between devices with their start and end apart: 9 -> 9, of which waited for: 5 -> 5; matrix products, arithmetic and copies ran while one was open for 7% -> 7% of each run, Pallas kernels for 16% -> 17%
where the time goes in v5:
time: 103 us
  waiting for transfers between devices  42.7 us (41%)
  starting transfers between devices  30.1 us (29%)
  Pallas kernels  20.7 us (20%)
  local copies, waits for them, and re-layouts  6.78 us (7%)
  other arithmetic  2.05 us (2%)
    pallas_call x1, Pallas kernels, attention_grads(): pl.pallas_call(attention_kernel, out_shape=(jax.ShapeDtypeStruct((spans *...  16.9 us
    all_to_all x1, waiting for transfers between devices, on_device(): lax.all_to_all(dkv.reshape(chips, tokens, -1), 'ctx', 0, 0, axis_index_gr...  15.5 us
    all_to_all x1, waiting for transfers between devices, on_device(): lax.all_to_all(to_all(keys_values, chips), 'ctx', 0, 0, axis_index_groups...  10.8 us
    all_to_all x1, starting transfers between devices, on_device(): lax.all_to_all(to_all(keys_values, chips), 'ctx', 0, 0, axis_index_groups...  9.6 us
    all_to_all x1, starting transfers between devices, on_device(): all_groups = lax.all_to_all(to_all(kv_grad, groups), 'tp', 0, 0)  7.8 us
    all_to_all x1, waiting for transfers between devices, on_device(): all_groups = lax.all_to_all(to_all(kv_grad, groups), 'tp', 0, 0)  7.64 us
    all_to_all x1, waiting for transfers between devices, on_device(): w_mine = lax.all_to_all(w_part, 'tp', 0, 0)  7.34 us
    all_to_all x1, starting transfers between devices, on_device(): w_mine = lax.all_to_all(w_part, 'tp', 0, 0)  6.64 us
  transfers between devices with their start and end apart: 9, of which 5 were waited for; matrix products, arithmetic and copies ran while one was open for 7% of the time, Pallas kernels for 17%

profile of v5, /device:TPU:32, one launch (start us, length us, event | category | flops | bytes accessed | tf_op | source)
XLA Modules:
  0.0 103.2 jit_solution(14373259110880020310)
XLA Ops:
  0.7 1.7 %broadcast_in_dim.6 = bf16[16,128,128]{2,1,0:T(8,128)(2,1)} broadcast(bf16[128,128]{1,0:T(8,128)(2,1)} %param.7), dimensions={1,2} | broadcast | bytes 557056 | tf_op jit(solution)/shard_map/broadcast_in_dim | solution.py:367
  2.4 9.6 %all-to-all-start = ((bf16[16,128,128]{2,1,0:T(8,128)(2,1)}), bf16[16,128,128]{2,1,0:T(8,128)(2,1)S(1)}, u32[]{:S(2)}, u32[]{:S(2)}) async-start(bf16[16,128,128]{2,1,0:T(8,128)(2,1)} %broadcast_in_dim.6), calls=%async_computation | async-start | bytes 1048576 | tf_op jit(solution)/shard_map/all_to_all | solution.py:372
  12.0 1.0 constant_dynamic-slice_fusion.2
  13.0 0.1 collective-permute-start
  13.2 2.9 %dynamic-slice_bitcast_fusion = bf16[8,928,128]{2,1,0:T(8,128)(2,1)} fusion(bf16[8,2,928,128]{3,2,1,0:T(8,128)(2,1)} %bitcast.16, s32[]{:T(128)S(6)} %select_n.51), kind=kLoop, calls=%fused_computation | loop fusion | bytes 3801092 | tf_op jit(solution)/shard_map/jit(dynamic_index_in_dim)/squeeze | solution.py:375
  16.1 10.8 %all-to-all-done = bf16[16,128,128]{2,1,0:T(8,128)(2,1)S(1)} async-done(((bf16[16,128,128]{2,1,0:T(8,128)(2,1)}), bf16[16,128,128]{2,1,0:T(8,128)(2,1)S(1)}, u32[]{:S(2)}, u32[]{:S(2)}) %all-to-all-start) | async-done | bytes 524320 | tf_op jit(solution)/shard_map/all_to_all | solution.py:372
  26.9 6.6 %all-to-all-start.1 = ((bf16[8,928,128]{2,1,0:T(8,128)(2,1)}), bf16[8,928,128]{2,1,0:T(8,128)(2,1)S(1)}, u32[]{:S(2)}, u32[]{:S(2)}) async-start(bf16[8,928,128]{2,1,0:T(8,128)(2,1)} %dynamic-slice_bitcast_fusion), calls=%async_computation.1 | async-start | bytes 3801088 | tf_op jit(solution)/shard_map/all_to_all | solution.py:386
  33.6 0.1 reshape.33
  33.9 0.1 reshape.34
  34.0 0.1 collective-permute-start.1
  34.3 0.3 shard_map.77
  34.6 1.4 %collective-permute-done.1 = bf16[16,128,128]{2,1,0:T(8,128)(2,1)S(1)} collective-permute-done((bf16[16,128,128]{2,1,0:T(8,128)(2,1)S(1)}, bf16[16,128,128]{2,1,0:T(8,128)(2,1)S(1)}, u32[]{:S(2)}, u32[]{:S(2)}) %collective-permute-start.1) | collective-permute-done | bytes 524320 | tf_op jit(solution)/shard_map/ppermute | solution.py:370
  36.0 16.9 %shard_map.78 = (bf16[256,512]{1,0:T(8,128)(2,1)S(1)}, bf16[32,64,128]{2,1,0:T(8,128)(2,1)S(1)}, bf16[32,64,128]{2,1,0:T(8,128)(2,1)}) custom-call(s32[64]{0:T(128)S(1)} %pad_add_fusion.slot_pos, s32[4]{0:T(128)S(1)} %pad_add_fusion.1.my_pos, bf16[32,64,128]{2,1,0:T(8,128)(2,1)S(1)} %bitcast.14, bf16[32,64,128]{2,1,0:T(8,128)(2,1)S(1)} %bitcast.15, ...), custom_call_target="tpu_custom_call" | custom-call | flops 1048576 | bytes 65536 | tf_op jit(solution)/shard_map/pallas_call | solution.py:298
  52.9 0.1 collective-permute-start.3
  53.0 7.3 %all-to-all-done.1.w_mine = bf16[8,928,128]{2,1,0:T(8,128)(2,1)S(1)} async-done(((bf16[8,928,128]{2,1,0:T(8,128)(2,1)}), bf16[8,928,128]{2,1,0:T(8,128)(2,1)S(1)}, u32[]{:S(2)}, u32[]{:S(2)}) %all-to-all-start.1) | async-done | bytes 1900576 | tf_op jit(solution)/shard_map/all_to_all | solution.py:386
  60.4 1.0 add_convert_fusion
  61.3 5.7 %all-to-all-start.2 = ((bf16[16,128,128]{2,1,0:T(8,128)(2,1)}), bf16[16,128,128]{2,1,0:T(8,128)(2,1)S(1)}, u32[]{:S(2)}, u32[]{:S(2)}) async-start(bf16[16,128,128]{2,1,0:T(8,128)(2,1)} %bitcast.7), calls=%async_computation.2 | async-start | bytes 1048576 | tf_op jit(solution)/shard_map/all_to_all | solution.py:409
  67.0 0.1 collective-permute-start.2
  67.1 15.5 %all-to-all-done.2 = bf16[16,128,128]{2,1,0:T(8,128)(2,1)S(1)} async-done(((bf16[16,128,128]{2,1,0:T(8,128)(2,1)}), bf16[16,128,128]{2,1,0:T(8,128)(2,1)S(1)}, u32[]{:S(2)}, u32[]{:S(2)}) %all-to-all-start.2) | async-done | bytes 524320 | tf_op jit(solution)/shard_map/all_to_all | solution.py:409
  82.8 0.7 broadcast_in_dim.8
  83.5 7.8 %all-to-all-start.3 = ((bf16[8,128,128]{2,1,0:T(8,128)(2,1)}), bf16[8,128,128]{2,1,0:T(8,128)(2,1)S(1)}, u32[]{:S(2)}, u32[]{:S(2)}) async-start(bf16[8,128,128]{2,1,0:T(8,128)(2,1)} %broadcast_in_dim.8), calls=%async_computation.3 | async-start | bytes 524288 | tf_op jit(solution)/shard_map/all_to_all | solution.py:413
  91.3 0.8 maximum_select_fusion
  92.1 7.6 %all-to-all-done.3.kv = bf16[8,128,128]{2,1,0:T(8,128)(2,1)S(1)} async-done(((bf16[8,128,128]{2,1,0:T(8,128)(2,1)}), bf16[8,128,128]{2,1,0:T(8,128)(2,1)S(1)}, u32[]{:S(2)}, u32[]{:S(2)}) %all-to-all-start.3) | async-done | bytes 262176 | tf_op jit(solution)/shard_map/all_to_all | solution.py:413
  99.7 3.5 %shard_map.79 = bf16[1856,128]{1,0:T(8,128)(2,1)} custom-call(s32[1]{0:T(128)} %bitcast.6.core, bf16[8,128,128]{2,1,0:T(8,128)(2,1)S(1)} %all-to-all-done.3.kv, bf16[8,928,128]{2,1,0:T(8,128)(2,1)S(1)} %all-to-all-done.1.w_mine, bf16[8,928,128]{2,1,0:T(8,128)(2,1)} %collective-permute-done.4.w_other), custom_call_target="tpu_custom_call" | custom-call | flops 486539264 | bytes 3801088 | tf_op jit(solution)/shard_map/pallas_call | solution.py:342
  (21 shorter events, 0.5 us)
Async XLA Ops:
  0.6 12.3 %copy-start = (bf16[128,1024]{1,0:T(8,128)(2,1)S(1)}, bf16[128,1024]{1,0:T(8,128)(2,1)}, u32[]{:S(2)}) copy-start(bf16[128,1024]{1,0:T(8,128)(2,1)} %param.8) | copy-start | bytes 786436
  0.6 12.3 %copy-start.1 = (bf16[128,1024]{1,0:T(8,128)(2,1)S(1)}, bf16[128,1024]{1,0:T(8,128)(2,1)}, u32[]{:S(2)}) copy-start(bf16[128,1024]{1,0:T(8,128)(2,1)} %param.9) | copy-start | bytes 786436
  2.4 24.6 %all-to-all-start = ((bf16[16,128,128]{2,1,0:T(8,128)(2,1)}), bf16[16,128,128]{2,1,0:T(8,128)(2,1)S(1)}, u32[]{:S(2)}, u32[]{:S(2)}) async-start(bf16[16,128,128]{2,1,0:T(8,128)(2,1)} %broadcast_in_dim.6), calls=%async_computation | async-start | bytes 1048576 | tf_op jit(solution)/shard_map/all_to_all | solution.py:372
  13.0 3.0 %collective-permute-start = (bf16[128,1536]{1,0:T(8,128)(2,1)S(1)}, bf16[128,1536]{1,0:T(8,128)(2,1)S(1)}, u32[]{:S(2)}, u32[]{:S(2)}) collective-permute-start(bf16[128,1536]{1,0:T(8,128)(2,1)S(1)} %pad_maximum_fusion), channel_id=1, source_target_pairs={{0,8},{8,0},{16,24},{24,16},{32,40},{40,32},{48,56},{56,48},{64,72... | collective-permute-start | bytes 1179656 | tf_op jit(solution)/shard_map/ppermute | solution.py:370
  16.1 17.5 %copy-start.2 = (s32[64]{0:T(128)S(1)}, s32[64]{0:T(128)}, u32[]{:S(2)}) copy-start(s32[64]{0:T(128)} %param.11) | copy-start | bytes 772
  26.9 33.4 %all-to-all-start.1 = ((bf16[8,928,128]{2,1,0:T(8,128)(2,1)}), bf16[8,928,128]{2,1,0:T(8,128)(2,1)S(1)}, u32[]{:S(2)}, u32[]{:S(2)}) async-start(bf16[8,928,128]{2,1,0:T(8,128)(2,1)} %dynamic-slice_bitcast_fusion), calls=%async_computation.1 | async-start | bytes 3801088 | tf_op jit(solution)/shard_map/all_to_all | solution.py:386
  34.0 2.0 %collective-permute-start.1 = (bf16[16,128,128]{2,1,0:T(8,128)(2,1)S(1)}, bf16[16,128,128]{2,1,0:T(8,128)(2,1)S(1)}, u32[]{:S(2)}, u32[]{:S(2)}) collective-permute-start(bf16[16,128,128]{2,1,0:T(8,128)(2,1)S(1)} %all-to-all-done), channel_id=1, source_target_pairs={{0,8},{8,0},{16,24},{24,16},{32,40},{40,32},{48,56},{56,48},{64,72... | collective-permute-start | bytes 1572872 | tf_op jit(solution)/shard_map/ppermute | solution.py:370
  52.9 7.5 %collective-permute-start.3 = (bf16[32,64,128]{2,1,0:T(8,128)(2,1)}, bf16[32,64,128]{2,1,0:T(8,128)(2,1)S(1)}, u32[]{:S(2)}, u32[]{:S(2)}) collective-permute-start(bf16[32,64,128]{2,1,0:T(8,128)(2,1)} %get-tuple-element.20), channel_id=1, source_target_pairs={{0,8},{8,0},{16,24},{24,16},{32,40},{40,32},{48,56},{56,48},{64,72... | collective-permute-start | bytes 1572872 | tf_op jit(solution)/shard_map/ppermute | solution.py:370
  60.3 39.4 %collective-permute-start.4 = (bf16[8,928,128]{2,1,0:T(8,128)(2,1)S(1)}, bf16[8,928,128]{2,1,0:T(8,128)(2,1)}, u32[]{:S(2)}, u32[]{:S(2)}) collective-permute-start(bf16[8,928,128]{2,1,0:T(8,128)(2,1)S(1)} %all-to-all-done.1.w_mine), channel_id=1, source_target_pairs={{0,8},{8,0},{16,24},{24,16},{32,40},{40,32},{48,56},{56,48},{64,72... | collective-permute-start | bytes 5701640 | tf_op jit(solution)/shard_map/ppermute | solution.py:370
  61.3 21.3 %all-to-all-start.2 = ((bf16[16,128,128]{2,1,0:T(8,128)(2,1)}), bf16[16,128,128]{2,1,0:T(8,128)(2,1)S(1)}, u32[]{:S(2)}, u32[]{:S(2)}) async-start(bf16[16,128,128]{2,1,0:T(8,128)(2,1)} %bitcast.7), calls=%async_computation.2 | async-start | bytes 1048576 | tf_op jit(solution)/shard_map/all_to_all | solution.py:409
  67.0 24.3 %collective-permute-start.2 = (bf16[128,512]{1,0:T(8,128)(2,1)S(1)}, bf16[128,512]{1,0:T(8,128)(2,1)S(1)}, u32[]{:S(2)}, u32[]{:S(2)}) collective-permute-start(bf16[128,512]{1,0:T(8,128)(2,1)S(1)} %get-tuple-element.25), channel_id=1, source_target_pairs={{0,8},{8,0},{16,24},{24,16},{32,40},{40,32},{48,56},{56,48},{64,72... | collective-permute-start | bytes 393224 | tf_op jit(solution)/shard_map/ppermute | solution.py:370
  83.5 16.2 %all-to-all-start.3 = ((bf16[8,128,128]{2,1,0:T(8,128)(2,1)}), bf16[8,128,128]{2,1,0:T(8,128)(2,1)S(1)}, u32[]{:S(2)}, u32[]{:S(2)}) async-start(bf16[8,128,128]{2,1,0:T(8,128)(2,1)} %broadcast_in_dim.8), calls=%async_computation.3 | async-start | bytes 524288 | tf_op jit(solution)/shard_map/all_to_all | solution.py:413
